TPU v7x, 128 devices: a whole 4x4x4 slice. The times are simulated.
128 devices in a mesh: rows: 64 (over z, x, y), rep: 2 (over core).
Axes of the slice: x: 4, y: 4, z: 4, core: 2. Of those that a mesh axis runs over, the one named last changes fastest.
Arguments:
- node_feats: bfloat16 [131072, 128], P('rows'), may hold values from -6 to 6
- w_in: bfloat16 [128, 256], replicated, may hold values from -0.5 to 0.5
- w_out: bfloat16 [256, 172], replicated
- labels: int32 [131072], P(('rows', 'rep')), may hold values from 0 to 171
- hub_rows: int32 [64, 2, 64], P('rows', 'rep'), may hold values from 0 to 2047, as said below
- send_rows: int32 [64, 2, 512], P('rows', 'rep'), may hold values from -1 to 2047, as said below
- adj_hub: bfloat16 [131072, 2, 4096], P('rows', 'rep'), may hold values from -0.0625 to 0.0625
- adj_sparse: bfloat16 [131072, 2, 512], P('rows', 'rep'), may hold values from -0.1875 to 0.1875
Outputs:
- logits: bfloat16 [131072, 172], P(('rows', 'rep'))
- grad_in: float32 [128, 256], replicated
- grad_out: float32 [256, 172], replicated
Inputs may be any that keep to these rules, and one draw needn't show every extreme that they name: `hub_rows`: within each owner slab the 2 x 64 hub nodes are distinct. `send_rows`: for each source, half and destination the live slots (not -1) come first; their count is 1 to 8, and for every source and half some destination has all 8 slots live. A node may fill several slots.
All inputs are finite; a program needn't handle non-finite values.
Results may differ from a plain program's by a relative error of at most 0.0095.
The roundings to bfloat16 on the way count: a program that leaves them out, or rounds other values in their place, can miss the bound.
Values may be sent and summed in bfloat16 or wider, within the bound.
No kernel may reach another device: no remote copies, remote signals or barrier semaphores. Data moves between devices by JAX's collectives and lax.ppermute only.
A program may use at most 128 MiB of HBM per device.

v0:
```python
import jax
import jax.numpy as jnp
from jax import lax
from jax.sharding import PartitionSpec as P


def on_device(node_feats, w_in, w_out, labels, hub_rows, send_rows, adj_hub, adj_sparse):
    high = lax.Precision.HIGHEST
    nrows = lax.axis_size("rows")
    slab = node_feats.shape[0]
    half = slab // lax.axis_size("rep")
    total_nodes = slab * nrows
    hub_local = hub_rows[0, 0]
    slot_local = send_rows[0, 0]
    hub_count = hub_local.shape[0]
    slot_count = slot_local.shape[0] // nrows
    hub_mat = adj_hub[:, 0, :]
    sparse_mat = adj_sparse[:, 0, :]
    own_start = lax.axis_index("rep") * half
    slab_iota = jnp.arange(slab, dtype=jnp.int32)

    def add_panel(piece):
        return jnp.dot(
            hub_mat, piece.reshape(-1, piece.shape[-1]), preferred_element_type=jnp.float32
        )

    def send_block(values):
        safe = jnp.maximum(slot_local, 0)
        picked = jnp.where((slot_local >= 0)[:, None], values[safe], jnp.zeros((), values.dtype))
        return picked.reshape(nrows, slot_count, values.shape[1])

    def slot_product(received):
        return jnp.dot(
            sparse_mat, received.reshape(-1, received.shape[-1]), preferred_element_type=jnp.float32
        )

    panel_in = node_feats[hub_local][None]
    hub_in = add_panel(lax.all_gather(panel_in, "rows", axis=0, tiled=True))
    got_in = lax.all_to_all(send_block(node_feats), "rows", split_axis=0, concat_axis=0, tiled=True)
    part_in = hub_in + slot_product(got_in)
    first_full = lax.psum(part_in, "rep").astype(jnp.bfloat16)
    pre_full = jnp.dot(first_full, w_in, preferred_element_type=jnp.float32)
    hidden = jnp.maximum(pre_full, 0.0).astype(jnp.bfloat16)
    first = lax.dynamic_slice_in_dim(first_full, own_start, half, 0)
    pre = lax.dynamic_slice_in_dim(pre_full, own_start, half, 0)
    panel_hidden = hidden[hub_local][None]
    hub_hidden = add_panel(lax.all_gather(panel_hidden, "rows", axis=0, tiled=True))
    got_hidden = lax.all_to_all(send_block(hidden), "rows", split_axis=0, concat_axis=0, tiled=True)
    part_hidden = hub_hidden + slot_product(got_hidden)
    second = lax.psum_scatter(part_hidden, "rep", scatter_dimension=0, tiled=True).astype(
        jnp.bfloat16
    )
    scores = jnp.dot(second, w_out, preferred_element_type=jnp.float32)
    classes = scores.shape[1]
    top = jnp.max(scores, axis=1, keepdims=True)
    expo = jnp.exp(scores - top)
    probs = expo / jnp.sum(expo, axis=1, keepdims=True)
    onehot = (labels[:, None] == jnp.arange(classes, dtype=jnp.int32)[None, :]).astype(jnp.float32)
    dscore = (probs - onehot) * (1.0 / jnp.sqrt(jnp.float32(total_nodes)))
    grad_out = jnp.dot(second.astype(jnp.float32).T, dscore, precision=high)
    hub_place = (hub_local[:, None] == slab_iota[None, :]).astype(jnp.float32)
    slot_place = (slot_local[:, None] == slab_iota[None, :]).astype(jnp.float32)
    sparse_wide = sparse_mat.astype(jnp.float32)
    w_back = w_out.astype(jnp.float32).T
    dsecond = jnp.dot(dscore, w_back, precision=high)
    dsecond_full = lax.all_gather(dsecond.astype(jnp.bfloat16), "rep", axis=0, tiled=True).astype(
        dsecond.dtype
    )

    def hub_term(start, count):
        columns = hub_mat.astype(jnp.float32)
        return jnp.dot(columns.T, dsecond_full, precision=high)

    hub_grad = (
        lambda term_fn: lax.psum_scatter(
            term_fn(jnp.int32(0), lax.axis_size("rows") * hub_count),
            "rows",
            scatter_dimension=0,
            tiled=True,
        )
    )(hub_term)
    slot_terms = jnp.dot(sparse_wide.T, dsecond_full, precision=high).reshape(
        nrows, slot_count, dsecond_full.shape[1]
    )
    returned = (
        lambda terms: lax.all_to_all(
            terms.astype(jnp.bfloat16), "rows", split_axis=0, concat_axis=0, tiled=True
        ).astype(terms.dtype)
    )(slot_terms)
    total = jnp.dot(hub_place.T, hub_grad, precision=high)
    part_back = total + jnp.dot(
        slot_place.T, returned.reshape(-1, dsecond_full.shape[1]), precision=high
    )
    dhidden = lax.psum_scatter(
        part_back.astype(jnp.bfloat16), "rep", scatter_dimension=0, tiled=True
    ).astype(jnp.float32)
    dpre = jnp.where(pre > 0, dhidden, jnp.zeros((), jnp.float32))
    grad_in = jnp.dot(first.astype(jnp.float32).T, dpre, precision=high)
    grad_in, grad_out = lax.psum((grad_in, grad_out), ("rows", "rep"))
    return (scores.astype(jnp.bfloat16), grad_in, grad_out)


def solution(mesh):
    return jax.shard_map(
        on_device,
        mesh=mesh,
        in_specs=(
            P("rows", None),
            P(),
            P(),
            P(("rows", "rep")),
            P("rows", "rep", None),
            P("rows", "rep", None),
            P("rows", "rep", None),
            P("rows", "rep", None),
        ),
        out_specs=(P(("rows", "rep"), None), P(), P()),
        check_vma=False,
    )
```

profile of v0, /device:TPU:0, one launch (start us, length us, event | category | flops | bytes accessed | tf_op | source)
XLA Modules:
  0.0 761.3 jit_solution(1166199465336886639)
XLA Ops:
  8.0 2.3 gather_fusion
  11.9 2.2 gather_fusion.1
  14.8 11.5 %all-to-all-start = ((bf16[64,8,128]{2,1,0:T(8,128)(2,1)}), bf16[64,8,128]{2,1,0:T(8,128)(2,1)S(1)}, u32[]{:S(2)}, u32[]{:S(2)}) async-start(bf16[64,8,128]{2,1,0:T(8,128)(2,1)} %bitcast_select_fusion.1), calls=%async_computation | async-start | bytes 262144 | tf_op jit(solution)/shard_map/all_to_all | solution.py:39
  26.4 51.6 %all-gather.8.cloned.1.call-done = bf16[4096,128]{1,0:T(8,128)(2,1)} async-done(((bf16[64,128]{1,0:T(8,128)(2,1)}), bf16[4096,128]{1,0:T(8,128)(2,1)}) %all-gather.8.cloned.1.call-update) | async-done | bytes 1048592 | tf_op jit(solution)/shard_map/all_gather | solution.py:38
  78.0 11.8 %fusion.4 = f32[128,2048]{1,0:T(8,128)S(1)} fusion(bf16[4096,128]{1,0:T(8,128)(2,1)} %all-gather.8.cloned.1.call-done, bf16[2048,1,4096]{2,0,1:T(8,128)(2,1)} %param.14), kind=kOutput, calls=%fused_computation.8 | convolution fusion | flops 2147483648 | bytes 18874368 | tf_op jit(solution)/shard_map/dot_general | solution.py:23
  89.9 1.8 fusion.13
  91.7 7.2 all-reduce.5
  98.9 2.9 maximum_convert_fusion
  101.8 1.3 gather_fusion.2
  103.1 2.0 gather_fusion.3
  105.9 6.5 all-to-all-start.1
  112.6 53.8 %all-gather.10.cloned.1.call-done = bf16[4096,256]{1,0:T(8,128)(2,1)} async-done(((bf16[64,256]{1,0:T(8,128)(2,1)}), bf16[4096,256]{1,0:T(8,128)(2,1)}) %all-gather.10.cloned.1.call-update) | async-done | bytes 2097168 | tf_op jit(solution)/shard_map/all_gather | solution.py:47
  166.4 12.3 %fusion.2 = f32[256,2048]{1,0:T(8,128)} fusion(bf16[4096,256]{1,0:T(8,128)(2,1)} %all-gather.10.cloned.1.call-done, bf16[2048,1,4096]{2,0,1:T(8,128)(2,1)} %param.14), kind=kOutput, calls=%fused_computation.6 | convolution fusion | flops 4294967296 | bytes 20971520 | tf_op jit(solution)/shard_map/dot_general | solution.py:23
  178.7 3.7 fusion.11
  182.5 9.8 %reduce-scatter.6.cloned.1.call-done = f32[1024,256]{0,1:T(8,128)} async-done(((f32[2048,256]{0,1:T(8,128)}), f32[1024,256]{0,1:T(8,128)}) %reduce-scatter.6.cloned.1.call-update) | async-done | bytes 1048592 | tf_op jit(solution)/shard_map/reduce_scatter | solution.py:50
  192.3 1.5 fusion.47
  193.8 0.8 fusion.28
  194.6 1.9 convolution_convert_fusion
  196.8 13.0 %all-gather.6.cloned.1.call-done = bf16[2048,256]{1,0:T(8,128)(2,1)} async-done(((bf16[1024,256]{1,0:T(8,128)(2,1)}), bf16[2048,256]{1,0:T(8,128)(2,1)}) %all-gather.6.cloned.1.call-update) | async-done | bytes 1048592 | tf_op jit(solution)/shard_map/all_gather | solution.py:66
  209.8 12.7 %fusion.6 = f32[4096,256]{0,1:T(8,128)} fusion(bf16[2048,256]{1,0:T(8,128)(2,1)} %all-gather.6.cloned.1.call-done, bf16[2048,1,4096]{2,0,1:T(8,128)(2,1)} %param.14), kind=kOutput, calls=%fused_computation.10 | convolution fusion | flops 4294967296 | bytes 22020096 | tf_op jit(solution)/shard_map/dot_general | solution.py:72
  222.5 5.6 copy.13
  228.1 2.0 fusion.22
  230.9 10.4 %all-to-all-start.2 = ((bf16[64,8,256]{2,1,0:T(8,128)(2,1)}), bf16[64,8,256]{2,1,0:T(8,128)(2,1)S(1)}, u32[]{:S(2)}, u32[]{:S(2)}) async-start(bf16[64,8,256]{2,1,0:T(8,128)(2,1)} %bitcast.15), calls=%async_computation.3 | async-start | bytes 524288 | tf_op jit(solution)/shard_map/all_to_all | solution.py:86
  241.4 346.0 %reduce-scatter.10.cloned.1.call-done = f32[64,256]{1,0:T(8,128)} async-done(((f32[4096,256]{1,0:T(8,128)}), f32[64,256]{1,0:T(8,128)}) %reduce-scatter.10.cloned.1.call-update) | async-done | bytes 65552
  587.4 3.3 fusion.31
  590.7 3.9 fusion.12
  594.7 2.7 fusion.37
  597.4 3.2 reduce-scatter.8.cloned.1.call-done
  600.6 2.6 fusion.25
  603.3 148.0 %all-reduce.4.cloned.1.call-done = (f32[128,256]{1,0:T(8,128)}, f32[256,172]{0,1:T(8,128)}) async-done(((f32[128,256]{1,0:T(8,128)}, f32[256,172]{0,1:T(8,128)}), (f32[128,256]{1,0:T(8,128)}, f32[256,172]{0,1:T(8,128)})) %all-reduce.4.cloned.1.call-update) | async-done | bytes 307216 | tf_op jit(solution)/shard_map/psum | solution.py:99
  751.3 1.6 copy.19
  752.9 1.6 copy.20
  (40 shorter events, 5.6 us)
Async XLA Ops:
  7.2 82.7 %copy-start = (bf16[2048,1,512]{2,0,1:T(8,128)(2,1)S(1)}, bf16[2048,1,512]{2,0,1:T(8,128)(2,1)}, u32[]{:S(2)}) copy-start(bf16[2048,1,512]{2,0,1:T(8,128)(2,1)} %param.15) | copy-start | bytes 6291460
  7.2 70.8 %all-gather.8.cloned.1.call-start = ((), (), s32[]{:S(2)}) async-start(), calls=%async_computation.9 | async-start | bytes 1064960 | tf_op jit(solution)/shard_map/all_gather | solution.py:38
  14.8 75.0 %all-to-all-start = ((bf16[64,8,128]{2,1,0:T(8,128)(2,1)}), bf16[64,8,128]{2,1,0:T(8,128)(2,1)S(1)}, u32[]{:S(2)}, u32[]{:S(2)}) async-start(bf16[64,8,128]{2,1,0:T(8,128)(2,1)} %bitcast_select_fusion.1), calls=%async_computation | async-start | bytes 262144 | tf_op jit(solution)/shard_map/all_to_all | solution.py:39
  26.3 140.1 %all-gather.10.cloned.1.call-start = ((), (), s32[]{:S(2)}) async-start(), calls=%async_computation.10 | async-start | bytes 2129920 | tf_op jit(solution)/shard_map/all_gather | solution.py:47
  89.8 9.1 %copy-start.3 = (bf16[128,256]{1,0:T(8,128)(2,1)S(1)}, bf16[128,256]{1,0:T(8,128)(2,1)}, u32[]{:S(2)}) copy-start(bf16[128,256]{1,0:T(8,128)(2,1)} %param.9) | copy-start | bytes 196612
  105.9 72.8 %all-to-all-start.1 = ((bf16[64,8,256]{2,1,0:T(8,128)(2,1)}), bf16[64,8,256]{2,1,0:T(8,128)(2,1)S(1)}, u32[]{:S(2)}, u32[]{:S(2)}) async-start(bf16[64,8,256]{2,1,0:T(8,128)(2,1)} %bitcast_select_fusion), calls=%async_computation.1 | async-start | bytes 524288 | tf_op jit(solution)/shard_map/all_to_all | solution.py:48
  112.4 79.9 %reduce-scatter.6.cloned.1.call-start = ((), (), s32[]{:S(2)}) async-start(), calls=%async_computation.6 | async-start | bytes 3145728 | tf_op jit(solution)/shard_map/reduce_scatter | solution.py:50
  182.4 9.9 %copy-start.2 = (bf16[256,172]{0,1:T(8,128)(2,1)S(1)}, bf16[256,172]{0,1:T(8,128)(2,1)}, u32[]{:S(2)}) copy-start(bf16[256,172]{0,1:T(8,128)(2,1)} %param.10) | copy-start | bytes 264196
  182.4 12.2 %copy-start.6 = (s32[1024]{0:T(1024)S(1)}, s32[1024]{0:T(1024)}, u32[]{:S(2)}) copy-start(s32[1024]{0:T(1024)} %param.11) | copy-start | bytes 12292
  182.4 27.4 %all-gather.6.cloned.1.call-start = ((), (), s32[]{:S(2)}) async-start(), calls=%async_computation.7 | async-start | bytes 1572864 | tf_op jit(solution)/shard_map/all_gather | solution.py:66
  196.5 390.9 %reduce-scatter.10.cloned.1.call-start = ((), (), s32[]{:S(2)}) async-start(), calls=%async_computation.11 | async-start | bytes 4259840
  228.1 359.3 %copy-start.5 = (s32[1,1,64]{2,1,0:T(1,128)S(1)}, s32[1,1,64]{2,1,0:T(1,128)}, u32[]{:S(2)}) copy-start(s32[1,1,64]{2,1,0:T(1,128)} %param.12) | copy-start | bytes 772
  230.1 360.6 %copy-start.4 = (s32[1,1,512]{2,1,0:T(1,128)S(1)}, s32[1,1,512]{2,1,0:T(1,128)}, u32[]{:S(2)}) copy-start(s32[1,1,512]{2,1,0:T(1,128)} %param.13) | copy-start | bytes 6148
  230.9 359.8 %all-to-all-start.2 = ((bf16[64,8,256]{2,1,0:T(8,128)(2,1)}), bf16[64,8,256]{2,1,0:T(8,128)(2,1)S(1)}, u32[]{:S(2)}, u32[]{:S(2)}) async-start(bf16[64,8,256]{2,1,0:T(8,128)(2,1)} %bitcast.15), calls=%async_computation.3 | async-start | bytes 524288 | tf_op jit(solution)/shard_map/all_to_all | solution.py:86
  241.3 359.3 %reduce-scatter.8.cloned.1.call-start = ((), (), s32[]{:S(2)}) async-start(), calls=%async_computation.8 | async-start | bytes 1572864 | tf_op jit(solution)/shard_map/reduce_scatter | solution.py:94
  594.6 6.0 copy-start.1
  594.7 156.6 %all-reduce.4.cloned.1.call-start = ((), (), s32[]{:S(2)}) async-start(), calls=%async_computation.12 | async-start | bytes 622592 | tf_op jit(solution)/shard_map/psum | solution.py:99
Sparse Core Ops, SparseCore 0:
  11.5 66.4 all-gather.7
  103.2 63.1 all-gather.9
  182.5 9.6 reduce-scatter.5
  196.6 13.1 all-gather.5
  228.2 359.1 reduce-scatter.9
  594.8 5.8 reduce-scatter.7
  606.9 144.3 all-reduce.3
where the time goes:
time: 764 us; the launch traced here: 761 us
  waiting for transfers between devices  626 us (82%)
  matrix products  63 us (8%)
  starting transfers between devices  29.1 us (4%)
  local copies, waits for them, and re-layouts  17.5 us (2%)
  between operations  14.3 us (2%)
    unnamed x8, waiting for transfers between devices  346 us
    psum x1, waiting for transfers between devices, on_device(): grad_in, grad_out = lax.psum((grad_in, grad_out), ('rows', 'rep'))  148 us
    all_gather x1, waiting for transfers between devices, on_device(): lax.all_gather(panel_hidden, 'rows', axis=0, tiled=True)  53.8 us
    all_gather x1, waiting for transfers between devices, on_device(): hub_in = add_panel(lax.all_gather(panel_in, 'rows', axis=0, tiled=True))  51.6 us
    dot_general x2, matrix products, add_panel(): jnp.dot(hub_mat, piece.reshape(-1, piece.shape[-1]), preferred_element_ty...  24.1 us
  transfers between devices with their start and end apart: 10, of which 7 were waited for; matrix products, arithmetic and copies ran while one was open for 5% of the time, Pallas kernels for 0%

commit v1 on v0

v1 whole, which is shorter than its diff:
```python
import jax
import jax.numpy as jnp
from jax import lax
from jax.sharding import PartitionSpec as P

SWAP = [(0, 1), (1, 0)]


def on_device(node_feats, w_in, w_out, labels, hub_rows, send_rows, adj_hub, adj_sparse):
    f32, bf16 = jnp.float32, jnp.bfloat16
    nrows = lax.axis_size("rows")
    slab = node_feats.shape[0]
    half = slab // lax.axis_size("rep")
    total_nodes = slab * nrows
    hub_local = hub_rows[0, 0]
    slot_local = send_rows[0, 0]
    hub_count = hub_local.shape[0]
    slot_count = slot_local.shape[0] // nrows
    hub_mat = adj_hub[:, 0, :]
    sparse_mat = adj_sparse[:, 0, :]
    core = lax.axis_index("rep")
    own_start = core * half
    oth_start = (1 - core) * half
    iota = jnp.arange(slab, dtype=jnp.int32)
    pick = (jnp.concatenate([hub_local, slot_local])[:, None] == iota[None, :]).astype(bf16)

    def dot(a, b):
        return jnp.dot(a, b, preferred_element_type=f32)

    def gather(values):
        rows = dot(pick, values).astype(bf16)
        width = rows.shape[1]
        hubs = jnp.broadcast_to(rows[:hub_count][None], (nrows, hub_count, width))
        slots = rows[hub_count:].reshape(nrows, slot_count, width)
        got = lax.all_to_all(
            jnp.concatenate([hubs, slots], axis=1), "rows", split_axis=0, concat_axis=0, tiled=True
        )
        return got[:, :hub_count].reshape(-1, width), got[:, hub_count:].reshape(-1, width)

    hub_x, slot_x = gather(node_feats)
    part = dot(hub_mat, hub_x) + dot(sparse_mat, slot_x)
    first = (part + lax.ppermute(part, "rep", SWAP)).astype(bf16)
    hub_f, slot_f = gather(first)
    hub_h = jnp.maximum(dot(hub_f, w_in), 0.0).astype(bf16)
    slot_h = jnp.maximum(dot(slot_f, w_in), 0.0).astype(bf16)
    part2 = dot(hub_mat, hub_h) + dot(sparse_mat, slot_h)
    away = lax.ppermute(lax.dynamic_slice_in_dim(part2, oth_start, half, 0), "rep", SWAP)
    second = (lax.dynamic_slice_in_dim(part2, own_start, half, 0) + away).astype(bf16)
    scores = dot(second, w_out)
    classes = scores.shape[1]
    top = jnp.max(scores, axis=1, keepdims=True)
    expo = jnp.exp(scores - top)
    probs = expo / jnp.sum(expo, axis=1, keepdims=True)
    onehot = (labels[:, None] == jnp.arange(classes, dtype=jnp.int32)[None, :]).astype(f32)
    dscore = (probs - onehot) * (1.0 / jnp.sqrt(f32(total_nodes)))
    high = dscore.astype(bf16)
    low = (dscore - high.astype(f32)).astype(bf16)
    grad_out_t = dot(high.T, second) + dot(low.T, second)
    dsec = dot(high, w_out.T).astype(bf16)
    dsec_away = lax.ppermute(dsec, "rep", SWAP)
    lower = jnp.where(core == 0, dsec, dsec_away)
    upper = jnp.where(core == 0, dsec_away, dsec)
    dfull = jnp.concatenate([lower, upper], axis=0)
    hub_d = jnp.where(hub_h > 0, dot(hub_mat.T, dfull), 0.0).astype(bf16)
    slot_d = jnp.where(slot_h > 0, dot(sparse_mat.T, dfull), 0.0).astype(bf16)
    grad_in = dot(hub_f.T, hub_d) + dot(slot_f.T, slot_d)

    flat = jnp.concatenate([grad_in, grad_out_t], axis=0)
    count, width = flat.shape
    share = -(-count // nrows)
    flat = jnp.pad(flat, ((0, share * nrows - count), (0, 0))).reshape(nrows, share, width)
    mine = lax.all_to_all(flat, "rows", split_axis=0, concat_axis=0, tiled=True).sum(axis=0)
    mine = mine + lax.ppermute(mine, "rep", SWAP)
    whole = lax.all_to_all(
        jnp.broadcast_to(mine[None], (nrows, share, width)), "rows", split_axis=0, concat_axis=0, tiled=True
    ).reshape(nrows * share, width)
    inner = w_in.shape[0]
    return (scores.astype(bf16), whole[:inner], whole[inner:count].T)


def solution(mesh):
    return jax.shard_map(
        on_device,
        mesh=mesh,
        in_specs=(
            P("rows", None),
            P(),
            P(),
            P(("rows", "rep")),
            P("rows", "rep", None),
            P("rows", "rep", None),
            P("rows", "rep", None),
            P("rows", "rep", None),
        ),
        out_specs=(P(("rows", "rep"), None), P(), P()),
        check_vma=False,
    )
```

time: 764 us -> 170 us (0.22)
  waiting for transfers between devices: 626 us -> 27.3 us
  blocking collectives: 7.24 us -> 68.1 us
  starting transfers between devices: 29.1 us -> 5.94 us
  between operations: 14.3 us -> 0.88 us
  local copies, waits for them, and re-layouts: 17.5 us -> 6.61 us
  matrix products: 63 us -> 54.6 us
    unnamed x8 -> x0, waiting for transfers between devices: 346 us -> none
    psum x1 -> x0, waiting for transfers between devices: 148 us -> none  [on_device(): grad_in, grad_out = lax.psum((grad_in, grad_out), ('rows', 'rep'))]
    all_gather x3 -> x0, waiting for transfers between devices: 118 us -> none  [the longest x1 53.8 us: on_device(): lax.all_gather(panel_hidden, 'rows', axis=0, tiled=True)]
    all_to_all x0 -> x3, blocking collectives: none -> 68.1 us  [the longest x1 31.4 us: gather(): lax.all_to_all(jnp.concatenate([hubs, slots], axis=1), 'rows', split_axis...]
    all_to_all x3 -> x1, starting transfers between devices: 28.4 us -> 5.33 us  [gather(): lax.all_to_all(jnp.concatenate([hubs, slots], axis=1), 'rows', split_axis...]
    all_to_all x3 -> x1, waiting for transfers between devices: 0.01 us -> 20.2 us  [gather(): lax.all_to_all(jnp.concatenate([hubs, slots], axis=1), 'rows', split_axis...]
    reduce_scatter x2 -> x0, waiting for transfers between devices: 13 us -> none  [the longest x1 9.81 us: on_device(): lax.psum_scatter(part_hidden, 'rep', scatter_dimension=0, tiled=True)]
    dot_general x13 -> x14, matrix products: 63 us -> 54.6 us  [dot(): return jnp.dot(a, b, preferred_element_type=f32)]
  transfers between devices with their start and end apart: 10 -> 5, of which waited for: 7 -> 5; matrix products, arithmetic and copies ran while one was open for 5% -> 1% of each run, Pallas kernels for 0% -> 0%
where the time goes in v1:
time: 170 us; the launch traced here: 169 us
  blocking collectives  68.1 us (40%)
  matrix products  54.6 us (32%)
  waiting for transfers between devices  27.3 us (16%)
  local copies, waits for them, and re-layouts  6.61 us (4%)
  starting transfers between devices  5.94 us (3%)
  other arithmetic  5.81 us (3%)
    dot_general x14, matrix products, dot(): return jnp.dot(a, b, preferred_element_type=f32)  54.6 us
    all_to_all x1, blocking collectives, gather(): lax.all_to_all(jnp.concatenate([hubs, slots], axis=1), 'rows', split_axis...  31.4 us
    all_to_all x1, waiting for transfers between devices, gather(): lax.all_to_all(jnp.concatenate([hubs, slots], axis=1), 'rows', split_axis...  20.2 us
    all_to_all x1, blocking collectives, on_device(): lax.all_to_all(flat, 'rows', split_axis=0, concat_axis=0, tiled=True)  18.5 us
    all_to_all x1, blocking collectives, on_device(): lax.all_to_all(jnp.broadcast_to(mine[None], (nrows, share, width)), 'rows...  18.2 us
    all_to_all x1, starting transfers between devices, gather(): lax.all_to_all(jnp.concatenate([hubs, slots], axis=1), 'rows', split_axis...  5.33 us
  transfers between devices with their start and end apart: 5, of which 5 were waited for; matrix products, arithmetic and copies ran while one was open for 1% of the time, Pallas kernels for 0%

profile of v1, /device:TPU:0, one launch (start us, length us, event | category | flops | bytes accessed | tf_op | source)
XLA Modules:
  0.0 169.2 jit_solution(5545034210787572241)
XLA Ops:
  0.6 0.9 pad_add_fusion
  1.6 1.9 %fusion.43 = bf16[576,128]{1,0:T(8,128)(2,1)S(1)} fusion(bf16[2048,128]{1,0:T(8,128)(2,1)} %param.8, s32[576]{0:T(1024)S(1)} %pad_add_fusion), kind=kOutput, calls=%fused_computation.35 | convolution fusion | flops 303243264 | bytes 674048 | tf_op jit(solution)/shard_map/dot_general | solution.py:28
  3.9 31.4 %all_to_all.20 = bf16[64,72,128]{2,1,0:T(8,128)(2,1)S(1)} all-to-all(bf16[64,72,128]{2,1,0:T(8,128)(2,1)S(1)} %pad_maximum_fusion), channel_id=1, replica_groups=mesh['rows'=64,'rep'=2] {'rows'}, dimensions={0} | all-to-all | bytes 2359296 | tf_op jit(solution)/shard_map/all_to_all | solution.py:35
  35.3 1.1 slice.42
  36.4 12.9 %fusion.4 = f32[128,2048]{1,0:T(8,128)} fusion(bf16[4096,128]{1,0:T(8,128)(2,1)} %bitcast.90, bf16[2048,1,4096]{2,0,1:T(8,128)(2,1)} %param.14), kind=kOutput, calls=%fused_computation.4 | convolution fusion | flops 2147483648 | bytes 18874368 | tf_op jit(solution)/shard_map/dot_general | solution.py:28
  49.2 2.0 %fusion.22 = f32[2048,128]{0,1:T(8,128)S(1)} fusion(f32[128,2048]{1,0:T(8,128)} %fusion.4, bf16[2048,1,512]{2,0,1:T(8,128)(2,1)S(1)} %copy-done, bf16[64,72,128]{2,1,0:T(8,128)(2,1)S(1)} %all_to_all.20), kind=kOutput, calls=%fused_computation.18 | convolution fusion | flops 268697600 | bytes 4325376 | tf_op jit(solution)/shard_map/dot_general | solution.py:28
  51.4 2.6 %collective-permute-done = f32[2048,128]{0,1:T(8,128)S(1)} collective-permute-done((f32[2048,128]{0,1:T(8,128)S(1)}, f32[2048,128]{0,1:T(8,128)S(1)}, u32[]{:S(2)}, u32[]{:S(2)}) %collective-permute-start) | collective-permute-done | bytes 1048608 | tf_op jit(solution)/shard_map/ppermute | solution.py:42
  54.0 0.9 fusion.44
  55.3 1.1 pad_maximum_fusion.1
  56.4 5.3 %all-to-all-start.1 = ((bf16[64,72,128]{2,1,0:T(8,128)(2,1)}), bf16[64,72,128]{2,1,0:T(8,128)(2,1)S(1)}, u32[]{:S(2)}, u32[]{:S(2)}) async-start(bf16[64,72,128]{2,1,0:T(8,128)(2,1)} %pad_maximum_fusion.1), calls=%async_computation.1 | async-start | bytes 2359296 | tf_op jit(solution)/shard_map/all_to_all | solution.py:35
  61.7 20.2 %all-to-all-done.1 = bf16[64,72,128]{2,1,0:T(8,128)(2,1)S(1)} async-done(((bf16[64,72,128]{2,1,0:T(8,128)(2,1)}), bf16[64,72,128]{2,1,0:T(8,128)(2,1)S(1)}, u32[]{:S(2)}, u32[]{:S(2)}) %all-to-all-start.1) | async-done | bytes 1179680 | tf_op jit(solution)/shard_map/all_to_all | solution.py:35
  82.1 1.0 copy-done.2
  83.0 2.0 %fusion.15 = bf16[4096,256]{1,0:T(8,128)(2,1)} fusion(bf16[4096,128]{1,0:T(8,128)(2,1)S(1)} %bitcast.88, bf16[128,256]{1,0:T(8,128)(2,1)S(1)} %copy-done.3), kind=kOutput, calls=%fused_computation.10 | convolution fusion | flops 270532608 | bytes 3211264 | tf_op jit(solution)/shard_map/dot_general | solution.py:28
  85.1 12.3 %fusion.2 = f32[256,2048]{1,0:T(8,128)} fusion(bf16[4096,256]{1,0:T(8,128)(2,1)} %fusion.15, bf16[2048,1,4096]{2,0,1:T(8,128)(2,1)} %param.14), kind=kOutput, calls=%fused_computation.2 | convolution fusion | flops 4294967296 | bytes 20971520 | tf_op jit(solution)/shard_map/dot_general | solution.py:28
  97.4 1.0 fusion.39
  98.4 2.4 %convolution_add_fusion = f32[256,2048]{1,0:T(8,128)S(1)} fusion(f32[256,2048]{1,0:T(8,128)} %fusion.2, bf16[512,256]{1,0:T(8,128)(2,1)S(1)} %fusion.39, bf16[2048,1,512]{2,0,1:T(8,128)(2,1)S(1)} %copy-done), kind=kOutput, calls=%fused_computation.16 | convolution fusion | flops 537395200 | bytes 6553600 | tf_op jit(solution)/shard_map/dot_general | solution.py:28
  100.8 1.3 copy-done.1
  102.1 1.1 dynamic-slice_bitcast_fusion
  103.2 3.0 %collective-permute-done.1 = f32[1024,256]{0,1:T(8,128)} collective-permute-done((f32[1024,256]{0,1:T(8,128)}, f32[1024,256]{0,1:T(8,128)}, u32[]{:S(2)}, u32[]{:S(2)}) %collective-permute-start.1) | collective-permute-done | bytes 1048608 | tf_op jit(solution)/shard_map/ppermute | solution.py:47
  106.1 1.7 fusion.48
  108.1 0.8 fusion.50
  109.0 0.5 convolution_convert_fusion
  109.4 0.4 collective-permute-start.2
  110.3 1.1 convolution_add_fusion.2
  111.6 1.1 broadcast_select_fusion.1
  112.7 2.9 %fusion.41 = f32[128,256]{1,0:T(8,128)} fusion(bf16[2048,1,512]{2,0,1:T(8,128)(2,1)S(1)} %copy-done, bf16[1024,256]{1,0:T(8,128)(2,1)} %get-tuple-element.4, bf16[1024,256]{1,0:T(8,128)(2,1)} %get-tuple-element.3, bf16[512,256]{1,0:T(8,128)(2,1)S(1)} %fusion.39, bf16[64,72,128]{2,1,0:T(8,128)(2,1)S(1)} %all-to-all-done.1), kind=kOutput, calls=%fused_computation.34 | convolution fusion | flops 572915712 | bytes 3670016 | tf_op jit(solution)/shard_map/dot_general | solution.py:28
  115.6 13.9 %fusion.45 = f32[128,256]{1,0:T(8,128)S(1)} fusion(f32[128,256]{1,0:T(8,128)} %fusion.41, bf16[4096,128]{1,0:T(8,128)(2,1)} %bitcast.89, bf16[2048,1,4096]{2,0,1:T(8,128)(2,1)} %param.14, bf16[4096,256]{1,0:T(8,128)(2,1)} %fusion.15, bf16[1024,256]{1,0:T(8,128)(2,1)} %get-tuple-element.4, bf16[1024,256]{1,0:T(8,128)(2,1)} %get-tuple-element.3), kind=kOutput, calls=%fused_computation.38 | convolution fusion | flops 4568678400 | bytes 21233664 | tf_op jit(solution)/shard_map/dot_general | solution.py:28
  129.6 18.5 %all_to_all.21 = f32[64,5,256]{2,1,0:T(8,128)S(1)} all-to-all(f32[64,5,256]{2,1,0:T(8,128)S(1)} %reshape.43), channel_id=1, replica_groups=mesh['rows'=64,'rep'=2] {'rows'}, dimensions={0} | all-to-all | bytes 655360 | tf_op jit(solution)/shard_map/all_to_all | solution.py:72
  148.3 1.2 collective-permute-done.3
  149.5 18.2 %all_to_all.22 = f32[64,5,256]{2,1,0:T(8,128)S(1)} all-to-all(f32[64,5,256]{2,1,0:T(8,128)S(1)} %broadcast_in_dim.10), channel_id=1, replica_groups=mesh['rows'=64,'rep'=2] {'rows'}, dimensions={0} | all-to-all | bytes 655360 | tf_op jit(solution)/shard_map/all_to_all | solution.py:74
  167.8 0.7 slice_bitcast_fusion
  168.5 0.7 slice.48
  (32 shorter events, 2.1 us)
Async XLA Ops:
  0.6 48.6 %copy-start = (bf16[2048,1,512]{2,0,1:T(8,128)(2,1)S(1)}, bf16[2048,1,512]{2,0,1:T(8,128)(2,1)}, u32[]{:S(2)}) copy-start(bf16[2048,1,512]{2,0,1:T(8,128)(2,1)} %param.15) | copy-start | bytes 6291460
  51.3 2.7 %collective-permute-start = (f32[2048,128]{0,1:T(8,128)S(1)}, f32[2048,128]{0,1:T(8,128)S(1)}, u32[]{:S(2)}, u32[]{:S(2)}) collective-permute-start(f32[2048,128]{0,1:T(8,128)S(1)} %fusion.22), channel_id=1, source_target_pairs={{0,1},{1,0},{2,3},{3,2},{4,5},{5,4},{6,7},{7,6},{8,9},{9,8},{10,11... | collective-permute-start | bytes 3145736 | tf_op jit(solution)/shard_map/ppermute | solution.py:42
  56.4 26.7 %copy-start.3 = (bf16[128,256]{1,0:T(8,128)(2,1)S(1)}, bf16[128,256]{1,0:T(8,128)(2,1)}, u32[]{:S(2)}) copy-start(bf16[128,256]{1,0:T(8,128)(2,1)} %param.9) | copy-start | bytes 196612
  56.4 25.5 %all-to-all-start.1 = ((bf16[64,72,128]{2,1,0:T(8,128)(2,1)}), bf16[64,72,128]{2,1,0:T(8,128)(2,1)S(1)}, u32[]{:S(2)}, u32[]{:S(2)}) async-start(bf16[64,72,128]{2,1,0:T(8,128)(2,1)} %pad_maximum_fusion.1), calls=%async_computation.1 | async-start | bytes 2359296 | tf_op jit(solution)/shard_map/all_to_all | solution.py:35
  82.1 1.0 copy-start.2
  100.8 1.3 copy-start.1
  103.1 3.0 %collective-permute-start.1 = (f32[1024,256]{0,1:T(8,128)}, f32[1024,256]{0,1:T(8,128)}, u32[]{:S(2)}, u32[]{:S(2)}) collective-permute-start(f32[1024,256]{0,1:T(8,128)} %dynamic-slice_bitcast_fusion), channel_id=1, source_target_pairs={{0,1},{1,0},{2,3},{3,2},{4,5},{5,4},{6,7},{7,6},{8,9},{9,8},{10,11... | collective-permute-start | bytes 3145736 | tf_op jit(solution)/shard_map/ppermute | solution.py:47
  103.1 4.7 %copy-start.5 = (bf16[256,172]{0,1:T(8,128)(2,1)S(1)}, bf16[256,172]{0,1:T(8,128)(2,1)}, u32[]{:S(2)}) copy-start(bf16[256,172]{0,1:T(8,128)(2,1)} %param.10) | copy-start | bytes 264196
  103.1 5.8 %copy-start.6 = (s32[1024]{0:T(1024)S(1)}, s32[1024]{0:T(1024)}, u32[]{:S(2)}) copy-start(s32[1024]{0:T(1024)} %param.11) | copy-start | bytes 12292
  109.4 2.2 %collective-permute-start.2 = (bf16[1024,256]{1,0:T(8,128)(2,1)S(1)}, bf16[1024,256]{1,0:T(8,128)(2,1)S(1)}, u32[]{:S(2)}, u32[]{:S(2)}) collective-permute-start(bf16[1024,256]{1,0:T(8,128)(2,1)S(1)} %convolution_convert_fusion), channel_id=1, source_target_pairs={{0,1},{1,0},{2,3},{3,2},{4,5},{5,4},{6,7},{7,6},{8,9},{9,8},{10,11... | collective-permute-start | bytes 1572872 | tf_op jit(solution)/shard_map/ppermute | solution.py:60
  115.6 13.9 %copy-start.4 = (f32[172,256]{1,0:T(8,128)S(1)}, f32[172,256]{1,0:T(8,128)}, u32[]{:S(2)}) copy-start(f32[172,256]{1,0:T(8,128)} %convolution_add_fusion.2) | copy-start | bytes 528388
  148.2 1.2 collective-permute-start.3

commit v2 on v1

v2 whole, which is shorter than its diff:
```python
import functools
import jax
import jax.numpy as jnp
from jax import lax
from jax.experimental import pallas as pl
from jax.experimental.pallas import tpu as pltpu
from jax.sharding import PartitionSpec as P

SWAP = [(0, 1), (1, 0)]
F32, BF16 = jnp.float32, jnp.bfloat16
VM = pl.BlockSpec(memory_space=pltpu.VMEM)
MIB = 1024 * 1024


def dot(a, b):
    return jnp.dot(a, b, preferred_element_type=F32)


def dot_t(a, b):
    return lax.dot_general(a, b, (((1,), (1,)), ((), ())), preferred_element_type=F32)


def call(body, outs, *args, flops=0, traffic=0, scratch=(), limit=16):
    return pl.pallas_call(
        body,
        out_shape=outs,
        in_specs=[VM] * len(args),
        out_specs=jax.tree.map(lambda _: VM, outs),
        scratch_shapes=scratch,
        compiler_params=pltpu.CompilerParams(vmem_limit_bytes=limit * MIB),
        cost_estimate=pl.CostEstimate(flops=flops, bytes_accessed=traffic, transcendentals=0),
    )(*args)


def one_hot(row, slab):
    count = row.shape[1]
    index = jnp.broadcast_to(row, (128, count)).T
    wide = jnp.concatenate([index] * (slab // 128), axis=1)
    return (wide == lax.broadcasted_iota(jnp.int32, (count, slab), 1)).astype(BF16)


def spread(values, hub_ref, slot_ref, out_ref):
    peers, rows, width = out_ref.shape
    hubs = hub_ref.shape[1]
    slab = values.shape[0]
    hub = dot(one_hot(hub_ref[...], slab), values)
    slot = dot(one_hot(slot_ref[...], slab), values)
    whole = jnp.concatenate(
        [
            jnp.broadcast_to(hub[None], (peers, hubs, width)),
            slot.reshape(peers, rows - hubs, width),
        ],
        axis=1,
    )
    out_ref[...] = whole.astype(BF16)


def pick_body(feat_ref, hub_ref, slot_ref, out_ref):
    spread(feat_ref[...], hub_ref, slot_ref, out_ref)


def pick_sum_body(part_ref, away_ref, hub_ref, slot_ref, out_ref):
    spread((part_ref[...] + away_ref[...]).astype(BF16), hub_ref, slot_ref, out_ref)


def split(got_ref, hubs):
    peers, rows, width = got_ref.shape
    hub = got_ref[:, :hubs, :].reshape(peers * hubs, width)
    slot = got_ref[:, hubs:, :].astype(F32).reshape(peers * (rows - hubs), width).astype(BF16)
    return hub, slot


def first_body(hubs, step, got_ref, hub_mat, sparse_mat, part_ref):
    hub, slot = split(got_ref, hubs)

    @pl.loop(0, part_ref.shape[0] // step)
    def _(i):
        at = pl.ds(pl.multiple_of(i * step, step), step)
        part_ref[at, :] = dot(hub_mat[at, :], hub) + dot(sparse_mat[at, :], slot)


def second_body(step, away, hid_hub, hid_slot, hub_mat, sparse_mat, part_ref):
    core = lax.axis_index("rep")
    start = (1 - core if away else core) * part_ref.shape[0]

    @pl.loop(0, part_ref.shape[0] // step)
    def _(i):
        at = pl.ds(pl.multiple_of(i * step, step), step)
        src = pl.ds(pl.multiple_of(start + i * step, step), step)
        part_ref[at, :] = dot(hub_mat[src, :], hid_hub[...]) + dot(sparse_mat[src, :], hid_slot[...])


def hidden_body(hubs, got_ref, w_ref, hub_out, slot_out):
    hub, slot = split(got_ref, hubs)
    hub_out[...] = jnp.maximum(dot(hub, w_ref[...]), 0.0).astype(BF16)
    slot_out[...] = jnp.maximum(dot(slot, w_ref[...]), 0.0).astype(BF16)


def score_body(scale, part_ref, away_ref, w_ref, label_ref, logit_ref, dsec_ref, grad_ref):
    second = (part_ref[...] + away_ref[...]).astype(BF16)
    scores = dot_t(w_ref[...], second)
    logit_ref[...] = scores.astype(BF16)
    top = jnp.max(scores, axis=0, keepdims=True)
    expo = jnp.exp(scores - top)
    probs = expo / jnp.sum(expo, axis=0, keepdims=True)
    hot = label_ref[...] == lax.broadcasted_iota(jnp.int32, scores.shape, 0)
    dscore = (probs - hot.astype(F32)) * scale
    high = dscore.astype(BF16)
    low = (dscore - high.astype(F32)).astype(BF16)
    grad_ref[...] = dot(high, second) + dot(low, second)
    dsec_ref[...] = lax.dot_general(
        w_ref[...], high, (((0,), (0,)), ((), ())), preferred_element_type=F32
    ).astype(BF16)


def back_body(hubs, step, own_ref, oth_ref, got_ref, w_ref, hub_mat, sparse_mat, grad_ref, dsec_ref, acc_ref):
    half = own_ref.shape[1]
    core = lax.axis_index("rep")
    w_t = w_ref[...].astype(F32).T.astype(BF16)
    peers, rows, width = got_ref.shape

    @pl.when(core == 0)
    def _():
        dsec_ref[:, :half] = own_ref[...]
        dsec_ref[:, half:] = oth_ref[...]

    @pl.when(core != 0)
    def _():
        dsec_ref[:, :half] = oth_ref[...]
        dsec_ref[:, half:] = own_ref[...]

    def term(cols, mat):
        hid = dot_t(w_t, cols)
        grad = jnp.where(hid > 0, dot(dsec_ref[...], mat), 0.0).astype(BF16)
        return dot(grad, cols)

    slot = got_ref[:, hubs:, :].astype(F32).reshape(peers * (rows - hubs), width).astype(BF16)
    acc_ref[...] = term(slot, sparse_mat[...])
    group = step // hubs

    @pl.loop(0, hub_mat.shape[1] // step)
    def _(i):
        at = pl.ds(pl.multiple_of(i * step, step), step)
        cols = got_ref[pl.ds(i * group, group), :hubs, :].reshape(step, width)
        acc_ref[...] += term(cols, hub_mat[:, at])

    grad_ref[...] = acc_ref[...].T


def on_device(node_feats, w_in, w_out, labels, hub_rows, send_rows, adj_hub, adj_sparse):
    nrows = lax.axis_size("rows")
    slab, width = node_feats.shape
    half = slab // lax.axis_size("rep")
    hid, classes = w_out.shape
    hubs = hub_rows.shape[2]
    slots = send_rows.shape[2] // nrows
    hub_cols, slot_cols = nrows * hubs, nrows * slots
    hub_row = hub_rows.reshape(1, hubs)
    slot_row = send_rows.reshape(1, slot_cols)
    hub_mat = pltpu.with_memory_space_constraint(adj_hub.reshape(slab, hub_cols), pltpu.VMEM)
    sparse_mat = pltpu.with_memory_space_constraint(adj_sparse.reshape(slab, slot_cols), pltpu.VMEM)
    shape = jax.ShapeDtypeStruct
    packet = shape((nrows, hubs + slots, width), BF16)
    products = 2 * slab * (hub_cols + slot_cols)

    def exchange(x):
        return lax.all_to_all(x, "rows", split_axis=0, concat_axis=0, tiled=True)

    def swap(x):
        return lax.ppermute(x, "rep", SWAP)

    got = exchange(call(pick_body, packet, node_feats, hub_row, slot_row, traffic=64 * MIB))
    part = call(
        functools.partial(first_body, hubs, 256), shape((slab, width), F32), got, hub_mat, sparse_mat,
        flops=products * width * 2,
    )
    got = exchange(call(pick_sum_body, packet, part, swap(part), hub_row, slot_row))
    hid_hub, hid_slot = call(
        functools.partial(hidden_body, hubs), (shape((hub_cols, hid), BF16), shape((slot_cols, hid), BF16)), got, w_in
    )

    def aggregate(away):
        return call(
            functools.partial(second_body, 256, away), shape((half, hid), F32), hid_hub, hid_slot, hub_mat, sparse_mat,
            flops=products * hid // 2,
        )

    away = swap(aggregate(True))
    part = aggregate(False)
    scale = float(1.0 / (slab * nrows) ** 0.5)
    logits, dsec, grad_out = call(
        functools.partial(score_body, scale),
        (shape((classes, half), BF16), shape((hid, half), BF16), shape((classes, hid), F32)),
        part, away, w_out.T, labels.reshape(1, half),
    )
    oth = swap(dsec)
    grad_in = call(
        functools.partial(back_body, hubs, 512), shape((width, hid), F32),
        dsec, oth, got, w_in, hub_mat, sparse_mat,
        scratch=[pltpu.VMEM((hid, slab), BF16), pltpu.VMEM((hid, width), F32)], flops=products * hid,
    )
    flat = jnp.concatenate([grad_in, grad_out], axis=0)
    count = width + classes
    share = -(-count // nrows)
    flat = jnp.pad(flat, ((0, share * nrows - count), (0, 0))).reshape(nrows, share, hid)
    mine = exchange(flat).sum(axis=0)
    mine = mine + swap(mine)
    whole = exchange(jnp.broadcast_to(mine[None], (nrows, share, hid))).reshape(nrows * share, hid)
    return (logits.T, whole[:width], whole[width:count].T)


def solution(mesh):
    return jax.shard_map(
        on_device,
        mesh=mesh,
        in_specs=(
            P("rows", None),
            P(),
            P(),
            P(("rows", "rep")),
            P("rows", "rep", None),
            P("rows", "rep", None),
            P("rows", "rep", None),
            P("rows", "rep", None),
        ),
        out_specs=(P(("rows", "rep"), None), P(), P()),
        check_vma=False,
    )
```

time: 170 us -> 136 us (0.80)
  matrix products: 54.6 us -> 0 us
  blocking collectives: 68.1 us -> 93.8 us
  Pallas kernels: 0 us -> 24.9 us
  waiting for transfers between devices: 27.3 us -> 5.35 us
  other arithmetic: 5.81 us -> 0.11 us
  starting transfers between devices: 5.94 us -> 0.74 us
  local copies, waits for them, and re-layouts: 6.61 us -> 9.68 us
    dot_general x14 -> x0, matrix products: 54.6 us -> none  [dot(): return jnp.dot(a, b, preferred_element_type=f32)]
    all_to_all x3 -> x4, blocking collectives: 68.1 us -> 93.8 us  [exchange(): return lax.all_to_all(x, 'rows', split_axis=0, concat_axis=0, tiled=True)]
    pallas_call x0 -> x8, Pallas kernels: none -> 24.9 us  [call(): pl.pallas_call(body, out_shape=outs, in_specs=[VM] * len(args), out_specs...]
    all_to_all x1 -> x0, waiting for transfers between devices: 20.2 us -> none  [gather(): lax.all_to_all(jnp.concatenate([hubs, slots], axis=1), 'rows', split_axis...]
    unnamed x14 -> x22, local copies, waits for them, and re-layouts: 2.29 us -> 8.18 us
    all_to_all x1 -> x0, starting transfers between devices: 5.33 us -> none  [gather(): lax.all_to_all(jnp.concatenate([hubs, slots], axis=1), 'rows', split_axis...]
    concatenate x4 -> x1, other arithmetic: 2.15 us -> 0.02 us  [on_device(): flat = jnp.concatenate([grad_in, grad_out], axis=0)]
    ppermute x4, waiting for transfers between devices: 7.06 us -> 5.35 us  [swap(): return lax.ppermute(x, 'rep', SWAP)]
  transfers between devices with their start and end apart: 5 -> 4, of which waited for: 5 -> 3; matrix products, arithmetic and copies ran while one was open for 1% -> 0% of each run, Pallas kernels for 0% -> 2%
where the time goes in v2:
time: 136 us; the launch traced here: 135 us
  blocking collectives  93.8 us (69%)
  Pallas kernels  24.9 us (18%)
  local copies, waits for them, and re-layouts  9.68 us (7%)
  waiting for transfers between devices  5.35 us (4%)
    all_to_all x4, blocking collectives, exchange(): return lax.all_to_all(x, 'rows', split_axis=0, concat_axis=0, tiled=True)  93.8 us
    pallas_call x8, Pallas kernels, call(): pl.pallas_call(body, out_shape=outs, in_specs=[VM] * len(args), out_specs...  24.9 us
    unnamed x22, local copies, waits for them, and re-layouts  8.18 us
    ppermute x4, waiting for transfers between devices, swap(): return lax.ppermute(x, 'rep', SWAP)  5.35 us
  transfers between devices with their start and end apart: 4, of which 3 were waited for; matrix products, arithmetic and copies ran while one was open for 0% of the time, Pallas kernels for 2%

profile of v2, /device:TPU:0, one launch (start us, length us, event | category | flops | bytes accessed | tf_op | source)
XLA Modules:
  0.0 135.4 jit_solution(7583821581918360508)
XLA Ops:
  0.6 1.0 copy-done.3
  1.7 0.7 copy-done.6
  2.4 0.7 copy-done.9
  3.0 0.9 shard_map.103
  4.0 0.0 copy-start.2
  4.0 31.5 %all_to_all.20.got_ref = bf16[64,72,128]{2,1,0:T(8,128)(2,1)S(1)} all-to-all(bf16[64,72,128]{2,1,0:T(8,128)(2,1)S(1)} %shard_map.103), channel_id=1, replica_groups=mesh['rows'=64,'rep'=2] {'rows'}, dimensions={0} | all-to-all | bytes 2359296 | tf_op jit(solution)/shard_map/all_to_all | solution.py:167
  35.5 5.8 %copy-done = bf16[2048,1,4096]{2,0,1:T(8,128)(2,1)S(1)} copy-done((bf16[2048,1,4096]{2,0,1:T(8,128)(2,1)S(1)}, bf16[2048,1,4096]{2,0,1:T(8,128)(2,1)}, u32[]{:S(2)}) %copy-start) | copy-done | bytes 16777240
  41.2 6.3 %shard_map.104.part_ref = f32[2048,128]{1,0:T(8,128)S(1)} custom-call(bf16[64,72,128]{2,1,0:T(8,128)(2,1)S(1)} %all_to_all.20.got_ref, bf16[2048,4096]{1,0:T(8,128)(2,1)S(1)} %bitcast.9, bf16[2048,512]{1,0:T(8,128)(2,1)S(1)} %bitcast.13), custom_call_target="tpu_custom_call" | custom-call | flops 4831838208 | tf_op jit(solution)/shard_map/pallas_call | solution.py:24
  47.5 0.1 collective-permute-start
  47.6 2.6 %collective-permute-done.away_ref = f32[2048,128]{1,0:T(8,128)S(1)} collective-permute-done((f32[2048,128]{1,0:T(8,128)S(1)}, f32[2048,128]{1,0:T(8,128)S(1)}, u32[]{:S(2)}, u32[]{:S(2)}) %collective-permute-start) | collective-permute-done | bytes 1048608 | tf_op jit(solution)/shard_map/ppermute | solution.py:170
  50.3 1.0 shard_map.105
  51.3 0.0 copy-start.4
  51.3 25.3 %all_to_all.21.got_ref = bf16[64,72,128]{2,1,0:T(8,128)(2,1)S(1)} all-to-all(bf16[64,72,128]{2,1,0:T(8,128)(2,1)S(1)} %shard_map.105), channel_id=1, replica_groups=mesh['rows'=64,'rep'=2] {'rows'}, dimensions={0} | all-to-all | bytes 2359296 | tf_op jit(solution)/shard_map/all_to_all | solution.py:167
  76.6 0.8 shard_map.106
  77.4 3.1 %shard_map.108 = f32[1024,256]{1,0:T(8,128)S(1)} custom-call(bf16[4096,256]{1,0:T(8,128)(2,1)S(1)} %get-tuple-element.8.hid_hub, bf16[512,256]{1,0:T(8,128)(2,1)S(1)} %get-tuple-element.9.hid_slot, bf16[2048,4096]{1,0:T(8,128)(2,1)S(1)} %bitcast.10, bf16[2048,512]{1,0:T(8,128)(2,1)S(1)} %bitcast.14), custom_call_target="tpu_custom_call" | custom-call | flops 2415919104 | tf_op jit(solution)/shard_map/pallas_call | solution.py:24
  80.5 0.0 copy-start.5
  80.5 0.0 copy-start.8
  80.5 0.1 collective-permute-start.1
  80.6 3.1 %shard_map.107.part_ref = f32[1024,256]{1,0:T(8,128)S(1)} custom-call(bf16[4096,256]{1,0:T(8,128)(2,1)S(1)} %get-tuple-element.8.hid_hub, bf16[512,256]{1,0:T(8,128)(2,1)S(1)} %get-tuple-element.9.hid_slot, bf16[2048,4096]{1,0:T(8,128)(2,1)S(1)} %bitcast.11, bf16[2048,512]{1,0:T(8,128)(2,1)S(1)} %bitcast.15), custom_call_target="tpu_custom_call" | custom-call | flops 2415919104 | tf_op jit(solution)/shard_map/pallas_call | solution.py:24
  83.8 1.2 shard_map.109
  84.9 0.5 collective-permute-start.2
  85.4 1.5 %collective-permute-done.2.oth_ref = bf16[256,1024]{1,0:T(8,128)(2,1)S(1)} collective-permute-done((bf16[256,1024]{1,0:T(8,128)(2,1)S(1)}, bf16[256,1024]{1,0:T(8,128)(2,1)S(1)}, u32[]{:S(2)}, u32[]{:S(2)}) %collective-permute-start.2) | collective-permute-done | bytes 524320 | tf_op jit(solution)/shard_map/ppermute | solution.py:170
  87.0 8.6 %shard_map.110 = f32[128,256]{1,0:T(8,128)S(1)} custom-call(bf16[256,1024]{1,0:T(8,128)(2,1)S(1)} %get-tuple-element.11.own_ref, bf16[256,1024]{1,0:T(8,128)(2,1)S(1)} %collective-permute-done.2.oth_ref, bf16[64,72,128]{2,1,0:T(8,128)(2,1)S(1)} %all_to_all.21.got_ref, bf16[128,256]{1,0:T(8,128)(2,1)S(1)} %copy-done.4, bf16[2048,4096]{1,0:T(8,128)(2,1)S(1)} %bitcast.12, ...), custom_call_target="tpu_custom_call" | custom-call | flops 4831838208 | tf_op jit(solution)/shard_map/pallas_call | solution.py:24
  95.6 0.1 reshape.33
  95.7 18.8 %all_to_all.22 = f32[64,5,256]{2,1,0:T(8,128)S(1)} all-to-all(f32[64,5,256]{2,1,0:T(8,128)S(1)} %reshape.33), channel_id=1, replica_groups=mesh['rows'=64,'rep'=2] {'rows'}, dimensions={0} | all-to-all | bytes 655360 | tf_op jit(solution)/shard_map/all_to_all | solution.py:167
  114.4 0.1 reduce_sum.9
  114.5 0.1 collective-permute-start.3
  114.6 1.2 collective-permute-done.3
  115.8 18.2 %all_to_all.23 = f32[64,5,256]{2,1,0:T(8,128)S(1)} all-to-all(f32[64,5,256]{2,1,0:T(8,128)S(1)} %broadcast_in_dim.2), channel_id=1, replica_groups=mesh['rows'=64,'rep'=2] {'rows'}, dimensions={0} | all-to-all | bytes 655360 | tf_op jit(solution)/shard_map/all_to_all | solution.py:167
  134.0 0.1 reshape.34
  134.1 0.7 slice.8
  134.7 0.7 slice_bitcast_fusion
  (18 shorter events, 0.1 us)
Async XLA Ops:
  0.6 1.0 copy-start.3
  1.7 0.7 copy-start.6
  2.4 0.7 copy-start.9
  4.0 31.5 %copy-start.2 = (bf16[2048,1,512]{2,0,1:T(8,128)(2,1)S(1)}, bf16[2048,1,512]{2,0,1:T(8,128)(2,1)}, u32[]{:S(2)}) copy-start(bf16[2048,1,512]{2,0,1:T(8,128)(2,1)} %param.15) | copy-start | bytes 6291460
  35.5 5.8 %copy-start = (bf16[2048,1,4096]{2,0,1:T(8,128)(2,1)S(1)}, bf16[2048,1,4096]{2,0,1:T(8,128)(2,1)}, u32[]{:S(2)}) copy-start(bf16[2048,1,4096]{2,0,1:T(8,128)(2,1)} %param.14) | copy-start | bytes 50331652
  41.2 9.0 %copy-start.7 = (s32[1,1,512]{2,1,0:T(1,128)S(1)}, s32[1,1,512]{2,1,0:T(1,128)}, u32[]{:S(2)}) copy-start(s32[1,1,512]{2,1,0:T(1,128)} %param.13) | copy-start | bytes 6148
  41.2 9.0 %copy-start.10 = (s32[1,1,64]{2,1,0:T(1,128)S(1)}, s32[1,1,64]{2,1,0:T(1,128)}, u32[]{:S(2)}) copy-start(s32[1,1,64]{2,1,0:T(1,128)} %param.12) | copy-start | bytes 772
  41.2 36.1 %copy-start.1 = (bf16[2048,1,4096]{2,0,1:T(8,128)(2,1)S(1)}, bf16[2048,1,4096]{2,0,1:T(8,128)(2,1)}, u32[]{:S(2)}) copy-start(bf16[2048,1,4096]{2,0,1:T(8,128)(2,1)} %param.14) | copy-start | bytes 50331652
  47.5 2.7 %collective-permute-start = (f32[2048,128]{1,0:T(8,128)S(1)}, f32[2048,128]{1,0:T(8,128)S(1)}, u32[]{:S(2)}, u32[]{:S(2)}) collective-permute-start(f32[2048,128]{1,0:T(8,128)S(1)} %shard_map.104.part_ref), channel_id=1, source_target_pairs={{0,1},{1,0},{2,3},{3,2},{4,5},{5,4},{6,7},{7,6},{8,9},{9,8},{10,11... | collective-permute-start | bytes 3145736 | tf_op jit(solution)/shard_map/ppermute | solution.py:170
  51.3 25.4 %copy-start.4 = (bf16[128,256]{1,0:T(8,128)(2,1)S(1)}, bf16[128,256]{1,0:T(8,128)(2,1)}, u32[]{:S(2)}) copy-start(bf16[128,256]{1,0:T(8,128)(2,1)} %w_ref.3) | copy-start | bytes 196612
  80.5 3.2 %copy-start.5 = (bf16[256,172]{0,1:T(8,128)(2,1)S(1)}, bf16[256,172]{0,1:T(8,128)(2,1)}, u32[]{:S(2)}) copy-start(bf16[256,172]{0,1:T(8,128)(2,1)} %param.10) | copy-start | bytes 264196
  80.5 3.2 %copy-start.8 = (s32[1024]{0:T(1024)S(1)}, s32[1024]{0:T(1024)}, u32[]{:S(2)}) copy-start(s32[1024]{0:T(1024)} %param.11) | copy-start | bytes 12292
  80.5 3.2 %collective-permute-start.1 = (f32[1024,256]{1,0:T(8,128)S(1)}, f32[1024,256]{1,0:T(8,128)S(1)}, u32[]{:S(2)}, u32[]{:S(2)}) collective-permute-start(f32[1024,256]{1,0:T(8,128)S(1)} %shard_map.108), channel_id=1, source_target_pairs={{0,1},{1,0},{2,3},{3,2},{4,5},{5,4},{6,7},{7,6},{8,9},{9,8},{10,11... | collective-permute-start | bytes 3145736 | tf_op jit(solution)/shard_map/ppermute | solution.py:170
  84.9 2.0 %collective-permute-start.2 = (bf16[256,1024]{1,0:T(8,128)(2,1)S(1)}, bf16[256,1024]{1,0:T(8,128)(2,1)S(1)}, u32[]{:S(2)}, u32[]{:S(2)}) collective-permute-start(bf16[256,1024]{1,0:T(8,128)(2,1)S(1)} %get-tuple-element.11.own_ref), channel_id=1, source_target_pairs={{0,1},{1,0},{2,3},{3,2},{4,5},{5,4},{6,7},{7,6},{8,9},{9,8},{10,11... | collective-permute-start | bytes 1572872 | tf_op jit(solution)/shard_map/ppermute | solution.py:170
  114.5 1.2 collective-permute-start.3

commit v3 on v2

--- a/solution.py
+++ b/solution.py
@@ -10,6 +10,9 @@
 F32, BF16 = jnp.float32, jnp.bfloat16
 VM = pl.BlockSpec(memory_space=pltpu.VMEM)
 MIB = 1024 * 1024
+STEP1 = 2048
+STEP2 = 1024
+STEP3 = 2048
 
 
 def dot(a, b):
@@ -55,8 +58,27 @@
     out_ref[...] = whole.astype(BF16)
 
 
-def pick_body(feat_ref, hub_ref, slot_ref, out_ref):
+def pick_body(feat_hbm, hub_hbm, slot_hbm, out_ref, feat_ref, hub_ref, slot_ref, sems):
+    pairs = ((hub_hbm, hub_ref), (slot_hbm, slot_ref), (feat_hbm, feat_ref))
+    copies = [pltpu.make_async_copy(src, dst, sems.at[i]) for i, (src, dst) in enumerate(pairs)]
+    for copy in copies:
+        copy.start()
+    for copy in copies:
+        copy.wait()
     spread(feat_ref[...], hub_ref, slot_ref, out_ref)
+
+
+def pick(packet, feats, hub_row, slot_row, flops):
+    return pl.pallas_call(
+        pick_body,
+        out_shape=packet,
+        in_specs=[pl.BlockSpec(memory_space=pl.ANY)] * 3,
+        out_specs=VM,
+        scratch_shapes=[pltpu.VMEM(x.shape, x.dtype) for x in (feats, hub_row, slot_row)]
+        + [pltpu.SemaphoreType.DMA((3,))],
+        compiler_params=pltpu.CompilerParams(vmem_limit_bytes=16 * MIB),
+        cost_estimate=pl.CostEstimate(flops=flops, bytes_accessed=0, transcendentals=0),
+    )(*(pltpu.with_memory_space_constraint(x, pltpu.HBM) for x in (feats, hub_row, slot_row)))
 
 
 def pick_sum_body(part_ref, away_ref, hub_ref, slot_ref, out_ref):
@@ -79,10 +101,7 @@
         part_ref[at, :] = dot(hub_mat[at, :], hub) + dot(sparse_mat[at, :], slot)
 
 
-def second_body(step, away, hid_hub, hid_slot, hub_mat, sparse_mat, part_ref):
-    core = lax.axis_index("rep")
-    start = (1 - core if away else core) * part_ref.shape[0]
-
+def second_rows(step, start, part_ref, hid_hub, hid_slot, hub_mat, sparse_mat):
     @pl.loop(0, part_ref.shape[0] // step)
     def _(i):
         at = pl.ds(pl.multiple_of(i * step, step), step)
@@ -90,10 +109,17 @@
         part_ref[at, :] = dot(hub_mat[src, :], hid_hub[...]) + dot(sparse_mat[src, :], hid_slot[...])
 
 
-def hidden_body(hubs, got_ref, w_ref, hub_out, slot_out):
+def away_body(hubs, step, got_ref, w_ref, hub_mat, sparse_mat, part_ref, hid_hub, hid_slot):
     hub, slot = split(got_ref, hubs)
-    hub_out[...] = jnp.maximum(dot(hub, w_ref[...]), 0.0).astype(BF16)
-    slot_out[...] = jnp.maximum(dot(slot, w_ref[...]), 0.0).astype(BF16)
+    hid_hub[...] = jnp.maximum(dot(hub, w_ref[...]), 0.0).astype(BF16)
+    hid_slot[...] = jnp.maximum(dot(slot, w_ref[...]), 0.0).astype(BF16)
+    start = (1 - lax.axis_index("rep")) * part_ref.shape[0]
+    second_rows(step, start, part_ref, hid_hub, hid_slot, hub_mat, sparse_mat)
+
+
+def own_body(step, hid_hub, hid_slot, hub_mat, sparse_mat, part_ref):
+    start = lax.axis_index("rep") * part_ref.shape[0]
+    second_rows(step, start, part_ref, hid_hub, hid_slot, hub_mat, sparse_mat)
 
 
 def score_body(scale, part_ref, away_ref, w_ref, label_ref, logit_ref, dsec_ref, grad_ref):
@@ -113,21 +139,11 @@
     ).astype(BF16)
 
 
-def back_body(hubs, step, own_ref, oth_ref, got_ref, w_ref, hub_mat, sparse_mat, grad_ref, dsec_ref, acc_ref):
-    half = own_ref.shape[1]
-    core = lax.axis_index("rep")
+def back_rows(hubs, step, start, dsec_ref, got_ref, w_ref, hub_mat, sparse_mat, acc_ref):
+    half = dsec_ref.shape[1]
+    peers, rows, width = got_ref.shape
     w_t = w_ref[...].astype(F32).T.astype(BF16)
-    peers, rows, width = got_ref.shape
-
-    @pl.when(core == 0)
-    def _():
-        dsec_ref[:, :half] = own_ref[...]
-        dsec_ref[:, half:] = oth_ref[...]
-
-    @pl.when(core != 0)
-    def _():
-        dsec_ref[:, :half] = oth_ref[...]
-        dsec_ref[:, half:] = own_ref[...]
+    src = pl.ds(pl.multiple_of(start, half), half)
 
     def term(cols, mat):
         hid = dot_t(w_t, cols)
@@ -135,16 +151,38 @@
         return dot(grad, cols)
 
     slot = got_ref[:, hubs:, :].astype(F32).reshape(peers * (rows - hubs), width).astype(BF16)
-    acc_ref[...] = term(slot, sparse_mat[...])
+    acc_ref[...] = term(slot, sparse_mat[src, :])
     group = step // hubs
 
     @pl.loop(0, hub_mat.shape[1] // step)
     def _(i):
         at = pl.ds(pl.multiple_of(i * step, step), step)
         cols = got_ref[pl.ds(i * group, group), :hubs, :].reshape(step, width)
-        acc_ref[...] += term(cols, hub_mat[:, at])
-
-    grad_ref[...] = acc_ref[...].T
+        acc_ref[...] += term(cols, hub_mat[src, at])
+
+
+def back_own_body(hubs, step, dsec_ref, got_ref, w_ref, hub_mat, sparse_mat, acc_ref):
+    start = lax.axis_index("rep") * dsec_ref.shape[1]
+    back_rows(hubs, step, start, dsec_ref, got_ref, w_ref, hub_mat, sparse_mat, acc_ref)
+
+
+def back_away_body(hubs, step, own_ref, grad_ref, dsec_ref, got_ref, w_ref, hub_mat, sparse_mat, out_ref, acc_ref):
+    start = (1 - lax.axis_index("rep")) * dsec_ref.shape[1]
+    back_rows(hubs, step, start, dsec_ref, got_ref, w_ref, hub_mat, sparse_mat, acc_ref)
+    width = got_ref.shape[2]
+    classes = grad_ref.shape[0]
+    out_ref[:width, :] = (acc_ref[...] + own_ref[...]).T
+    out_ref[width : width + classes, :] = grad_ref[...]
+    rest = out_ref.shape[0] - width - classes
+    out_ref[width + classes :, :] = jnp.zeros((rest, out_ref.shape[1]), F32)
+
+
+def sum_body(got_ref, out_ref):
+    out_ref[...] = jnp.sum(got_ref[...], axis=0)
+
+
+def share_body(mine_ref, away_ref, out_ref):
+    out_ref[...] = jnp.broadcast_to((mine_ref[...] + away_ref[...])[None], out_ref.shape)
 
 
 def on_device(node_feats, w_in, w_out, labels, hub_rows, send_rows, adj_hub, adj_sparse):
@@ -169,24 +207,23 @@
     def swap(x):
         return lax.ppermute(x, "rep", SWAP)
 
-    got = exchange(call(pick_body, packet, node_feats, hub_row, slot_row, traffic=64 * MIB))
+    got = exchange(pick(packet, node_feats, hub_row, slot_row, products * 256))
     part = call(
-        functools.partial(first_body, hubs, 256), shape((slab, width), F32), got, hub_mat, sparse_mat,
+        functools.partial(first_body, hubs, STEP1), shape((slab, width), F32), got, hub_mat, sparse_mat,
         flops=products * width * 2,
     )
     got = exchange(call(pick_sum_body, packet, part, swap(part), hub_row, slot_row))
-    hid_hub, hid_slot = call(
-        functools.partial(hidden_body, hubs), (shape((hub_cols, hid), BF16), shape((slot_cols, hid), BF16)), got, w_in
-    )
-
-    def aggregate(away):
-        return call(
-            functools.partial(second_body, 256, away), shape((half, hid), F32), hid_hub, hid_slot, hub_mat, sparse_mat,
-            flops=products * hid // 2,
-        )
-
-    away = swap(aggregate(True))
-    part = aggregate(False)
+    part, hid_hub, hid_slot = call(
+        functools.partial(away_body, hubs, STEP2),
+        (shape((half, hid), F32), shape((hub_cols, hid), BF16), shape((slot_cols, hid), BF16)),
+        got, w_in, hub_mat, sparse_mat,
+        flops=products * hid // 2,
+    )
+    away = swap(part)
+    part = call(
+        functools.partial(own_body, STEP2), shape((half, hid), F32), hid_hub, hid_slot, hub_mat, sparse_mat,
+        flops=products * hid // 2,
+    )
     scale = float(1.0 / (slab * nrows) ** 0.5)
     logits, dsec, grad_out = call(
         functools.partial(score_body, scale),
@@ -194,18 +231,20 @@
         part, away, w_out.T, labels.reshape(1, half),
     )
     oth = swap(dsec)
-    grad_in = call(
-        functools.partial(back_body, hubs, 512), shape((width, hid), F32),
-        dsec, oth, got, w_in, hub_mat, sparse_mat,
-        scratch=[pltpu.VMEM((hid, slab), BF16), pltpu.VMEM((hid, width), F32)], flops=products * hid,
-    )
-    flat = jnp.concatenate([grad_in, grad_out], axis=0)
+    own = call(
+        functools.partial(back_own_body, hubs, STEP3), shape((hid, width), F32), dsec, got, w_in, hub_mat, sparse_mat,
+        flops=products * hid // 2,
+    )
     count = width + classes
-    share = -(-count // nrows)
-    flat = jnp.pad(flat, ((0, share * nrows - count), (0, 0))).reshape(nrows, share, hid)
-    mine = exchange(flat).sum(axis=0)
-    mine = mine + swap(mine)
-    whole = exchange(jnp.broadcast_to(mine[None], (nrows, share, hid))).reshape(nrows * share, hid)
+    share = -(-count // (8 * nrows)) * 8
+    flat = call(
+        functools.partial(back_away_body, hubs, STEP3), shape((share * nrows, hid), F32),
+        own, grad_out, oth, got, w_in, hub_mat, sparse_mat,
+        scratch=[pltpu.VMEM((hid, width), F32)], flops=products * hid // 2,
+    )
+    mine = call(sum_body, shape((share, hid), F32), exchange(flat.reshape(nrows, share, hid)))
+    whole = call(share_body, shape((nrows, share, hid), F32), mine, swap(mine))
+    whole = exchange(whole).reshape(nrows * share, hid)
     return (logits.T, whole[:width], whole[width:count].T)
 
 

time: 136 us -> 125 us (0.919)
  local copies, waits for them, and re-layouts: 9.68 us -> 1.38 us
  waiting for transfers between devices: 5.35 us -> 3.83 us
    unnamed x22 -> x14, local copies, waits for them, and re-layouts: 8.18 us -> 0.04 us
    pallas_call x8 -> x9, Pallas kernels: 24.9 us -> 22.4 us  [call(): pl.pallas_call(body, out_shape=outs, in_specs=[VM] * len(args), out_specs...]
    pallas_call x0 -> x1, Pallas kernels: none -> 2.19 us  [pick(): pl.pallas_call(pick_body, out_shape=packet, in_specs=[pl.BlockSpec(memory...]
    ppermute x4, waiting for transfers between devices: 5.35 us -> 3.83 us  [swap(): return lax.ppermute(x, 'rep', SWAP)]
  transfers between devices with their start and end apart: 4 -> 4, of which waited for: 3 -> 2; matrix products, arithmetic and copies ran while one was open for 0% -> 0% of each run, Pallas kernels for 2% -> 6%
where the time goes in v3:
time: 125 us
  blocking collectives  93.6 us (75%)
  Pallas kernels  24.6 us (20%)
  waiting for transfers between devices  3.83 us (3%)
  local copies, waits for them, and re-layouts  1.38 us (1%)
    all_to_all x4, blocking collectives, exchange(): return lax.all_to_all(x, 'rows', split_axis=0, concat_axis=0, tiled=True)  93.6 us
    pallas_call x9, Pallas kernels, call(): pl.pallas_call(body, out_shape=outs, in_specs=[VM] * len(args), out_specs...  22.4 us
    ppermute x4, waiting for transfers between devices, swap(): return lax.ppermute(x, 'rep', SWAP)  3.83 us
  transfers between devices with their start and end apart: 4, of which 2 were waited for; matrix products, arithmetic and copies ran while one was open for 0% of the time, Pallas kernels for 6%

profile of v3, /device:TPU:0, one launch (start us, length us, event | category | flops | bytes accessed | tf_op | source)
XLA Modules:
  0.0 125.1 jit_solution(10052242446808479223)
XLA Ops:
  0.6 0.0 copy-start
  0.6 2.2 %shard_map.103 = bf16[64,72,128]{2,1,0:T(8,128)(2,1)S(1)} custom-call(bf16[2048,128]{1,0:T(8,128)(2,1)} %feat_hbm.1, s32[1,64]{1,0:T(1,128)} %bitcast.28, s32[1,512]{1,0:T(1,128)} %bitcast.26), custom_call_target="tpu_custom_call" | custom-call | flops 4831838208 | tf_op jit(solution)/shard_map/pallas_call | solution.py:72
  2.8 0.0 copy-start.1
  2.8 31.6 %all_to_all.20.got_ref = bf16[64,72,128]{2,1,0:T(8,128)(2,1)S(1)} all-to-all(bf16[64,72,128]{2,1,0:T(8,128)(2,1)S(1)} %shard_map.103), channel_id=1, replica_groups=mesh['rows'=64,'rep'=2] {'rows'}, dimensions={0} | all-to-all | bytes 2359296 | tf_op jit(solution)/shard_map/all_to_all | solution.py:205
  34.5 0.0 copy-done
  34.5 0.0 copy-done.1
  34.5 5.1 %shard_map.104.part_ref = f32[2048,128]{1,0:T(8,128)S(1)} custom-call(bf16[64,72,128]{2,1,0:T(8,128)(2,1)S(1)} %all_to_all.20.got_ref, bf16[2048,4096]{1,0:T(8,128)(2,1)S(1)} %bitcast.13, bf16[2048,512]{1,0:T(8,128)(2,1)S(1)} %bitcast.18), custom_call_target="tpu_custom_call" | custom-call | flops 4831838208 | tf_op jit(solution)/shard_map/pallas_call | solution.py:27
  39.6 0.1 collective-permute-start
  39.7 2.6 %collective-permute-done.away_ref = f32[2048,128]{1,0:T(8,128)S(1)} collective-permute-done((f32[2048,128]{1,0:T(8,128)S(1)}, f32[2048,128]{1,0:T(8,128)S(1)}, u32[]{:S(2)}, u32[]{:S(2)}) %collective-permute-start) | collective-permute-done | bytes 1048608 | tf_op jit(solution)/shard_map/ppermute | solution.py:208
  42.3 0.0 copy-done.5
  42.3 1.0 shard_map.105
  43.3 0.0 copy-start.2
  43.3 25.4 %all_to_all.21.got_ref = bf16[64,72,128]{2,1,0:T(8,128)(2,1)S(1)} all-to-all(bf16[64,72,128]{2,1,0:T(8,128)(2,1)S(1)} %shard_map.105), channel_id=1, replica_groups=mesh['rows'=64,'rep'=2] {'rows'}, dimensions={0} | all-to-all | bytes 2359296 | tf_op jit(solution)/shard_map/all_to_all | solution.py:205
  68.7 3.7 %shard_map.106 = (f32[1024,256]{1,0:T(8,128)S(1)}, bf16[4096,256]{1,0:T(8,128)(2,1)S(1)}, bf16[512,256]{1,0:T(8,128)(2,1)S(1)}) custom-call(bf16[64,72,128]{2,1,0:T(8,128)(2,1)S(1)} %all_to_all.21.got_ref, bf16[128,256]{1,0:T(8,128)(2,1)S(1)} %copy-done.2, bf16[2048,4096]{1,0:T(8,128)(2,1)S(1)} %bitcast.14, bf16[2048,512]{1,0:T(8,128)(2,1)S(1)} %bitcast.19), custom_call_target="tpu_custom_call" | custom-call | flops 2415919104 | tf_op jit(solution)/shard_map/pallas_call | solution.py:27
  72.3 0.3 collective-permute-start.1
  72.6 0.0 copy-start.3
  72.6 0.0 copy-start.4
  72.6 2.6 %shard_map.107.part_ref = f32[1024,256]{1,0:T(8,128)S(1)} custom-call(bf16[4096,256]{1,0:T(8,128)(2,1)S(1)} %get-tuple-element.9.hid_hub, bf16[512,256]{1,0:T(8,128)(2,1)S(1)} %get-tuple-element.10.hid_slot, bf16[2048,4096]{1,0:T(8,128)(2,1)S(1)} %bitcast.15, bf16[2048,512]{1,0:T(8,128)(2,1)S(1)} %bitcast.20), custom_call_target="tpu_custom_call" | custom-call | flops 2415919104 | tf_op jit(solution)/shard_map/pallas_call | solution.py:27
  75.2 0.0 collective-permute-done.1.away_ref
  75.3 0.0 copy-done.4
  75.3 1.2 shard_map.108
  76.4 0.5 collective-permute-start.2
  76.9 4.3 %shard_map.109.own_ref = f32[256,128]{1,0:T(8,128)S(1)} custom-call(bf16[256,1024]{1,0:T(8,128)(2,1)S(1)} %get-tuple-element.13.dsec_ref, bf16[64,72,128]{2,1,0:T(8,128)(2,1)S(1)} %all_to_all.21.got_ref, bf16[128,256]{1,0:T(8,128)(2,1)S(1)} %copy-done.2, bf16[2048,4096]{1,0:T(8,128)(2,1)S(1)} %bitcast.16, bf16[2048,512]{1,0:T(8,128)(2,1)S(1)} %bitcast.21), custom_call_target="tpu_custom_call" | custom-call | flops 2415919104 | tf_op jit(solution)/shard_map/pallas_call | solution.py:27
  81.3 0.0 collective-permute-done.2.dsec_ref
  81.3 4.5 %shard_map.110 = f32[512,256]{1,0:T(8,128)S(1)} custom-call(f32[256,128]{1,0:T(8,128)S(1)} %shard_map.109.own_ref, f32[172,256]{1,0:T(8,128)S(1)} %get-tuple-element.14.grad_ref, bf16[256,1024]{1,0:T(8,128)(2,1)S(1)} %collective-permute-done.2.dsec_ref, bf16[64,72,128]{2,1,0:T(8,128)(2,1)S(1)} %all_to_all.21.got_ref, bf16[128,256]{1,0:T(8,128)(2,1)S(1)} %copy-done.2, ...), custom_call_target="tpu_custom_call" | custom-call | flops 2415919104 | tf_op jit(solution)/shard_map/pallas_call | solution.py:27
  85.7 18.4 %all_to_all.22.got_ref = f32[64,8,256]{2,1,0:T(8,128)S(1)} all-to-all(f32[64,8,256]{2,1,0:T(8,128)S(1)} %bitcast.23), channel_id=1, replica_groups=mesh['rows'=64,'rep'=2] {'rows'}, dimensions={0} | all-to-all | bytes 1048576 | tf_op jit(solution)/shard_map/all_to_all | solution.py:205
  104.1 0.1 shard_map.111.mine_ref
  104.2 0.1 collective-permute-start.3
  104.3 1.2 collective-permute-done.3.away_ref
  105.5 18.2 %all_to_all.23 = f32[64,8,256]{2,1,0:T(8,128)S(1)} all-to-all(f32[64,8,256]{2,1,0:T(8,128)S(1)} %shard_map.112), channel_id=1, replica_groups=mesh['rows'=64,'rep'=2] {'rows'}, dimensions={0} | all-to-all | bytes 1048576 | tf_op jit(solution)/shard_map/all_to_all | solution.py:205
  123.7 0.7 slice_bitcast_fusion
  124.4 0.7 slice_bitcast_fusion.1
  (6 shorter events, 0.0 us)
Async XLA Ops:
  0.6 33.9 %copy-start = (bf16[2048,1,4096]{2,0,1:T(8,128)(2,1)S(1)}, bf16[2048,1,4096]{2,0,1:T(8,128)(2,1)}, u32[]{:S(2)}) copy-start(bf16[2048,1,4096]{2,0,1:T(8,128)(2,1)} %param.14) | copy-start | bytes 50331652
  2.8 31.7 %copy-start.1 = (bf16[2048,1,512]{2,0,1:T(8,128)(2,1)S(1)}, bf16[2048,1,512]{2,0,1:T(8,128)(2,1)}, u32[]{:S(2)}) copy-start(bf16[2048,1,512]{2,0,1:T(8,128)(2,1)} %param.15) | copy-start | bytes 6291460
  34.5 7.8 %copy-start.5 = (s32[1,1,512]{2,1,0:T(1,128)S(1)}, s32[1,1,512]{2,1,0:T(1,128)}, u32[]{:S(2)}) copy-start(s32[1,1,512]{2,1,0:T(1,128)} %param.13) | copy-start | bytes 6148
  34.5 7.8 %copy-start.6 = (s32[1,1,64]{2,1,0:T(1,128)S(1)}, s32[1,1,64]{2,1,0:T(1,128)}, u32[]{:S(2)}) copy-start(s32[1,1,64]{2,1,0:T(1,128)} %param.12) | copy-start | bytes 772
  39.6 2.7 %collective-permute-start = (f32[2048,128]{1,0:T(8,128)S(1)}, f32[2048,128]{1,0:T(8,128)S(1)}, u32[]{:S(2)}, u32[]{:S(2)}) collective-permute-start(f32[2048,128]{1,0:T(8,128)S(1)} %shard_map.104.part_ref), channel_id=1, source_target_pairs={{0,1},{1,0},{2,3},{3,2},{4,5},{5,4},{6,7},{7,6},{8,9},{9,8},{10,11... | collective-permute-start | bytes 3145736 | tf_op jit(solution)/shard_map/ppermute | solution.py:208
  43.3 25.4 %copy-start.2 = (bf16[128,256]{1,0:T(8,128)(2,1)S(1)}, bf16[128,256]{1,0:T(8,128)(2,1)}, u32[]{:S(2)}) copy-start(bf16[128,256]{1,0:T(8,128)(2,1)} %w_ref.5) | copy-start | bytes 196612
  72.3 2.9 %collective-permute-start.1 = (f32[1024,256]{1,0:T(8,128)S(1)}, f32[1024,256]{1,0:T(8,128)S(1)}, u32[]{:S(2)}, u32[]{:S(2)}) collective-permute-start(f32[1024,256]{1,0:T(8,128)S(1)} %get-tuple-element.11), channel_id=1, source_target_pairs={{0,1},{1,0},{2,3},{3,2},{4,5},{5,4},{6,7},{7,6},{8,9},{9,8},{10,11... | collective-permute-start | bytes 3145736 | tf_op jit(solution)/shard_map/ppermute | solution.py:208
  72.6 2.6 %copy-start.3 = (bf16[256,172]{0,1:T(8,128)(2,1)S(1)}, bf16[256,172]{0,1:T(8,128)(2,1)}, u32[]{:S(2)}) copy-start(bf16[256,172]{0,1:T(8,128)(2,1)} %param.10) | copy-start | bytes 264196
  72.6 2.6 %copy-start.4 = (s32[1024]{0:T(1024)S(1)}, s32[1024]{0:T(1024)}, u32[]{:S(2)}) copy-start(s32[1024]{0:T(1024)} %param.11) | copy-start | bytes 12292
  76.4 4.8 %collective-permute-start.2 = (bf16[256,1024]{1,0:T(8,128)(2,1)S(1)}, bf16[256,1024]{1,0:T(8,128)(2,1)S(1)}, u32[]{:S(2)}, u32[]{:S(2)}) collective-permute-start(bf16[256,1024]{1,0:T(8,128)(2,1)S(1)} %get-tuple-element.13.dsec_ref), channel_id=1, source_target_pairs={{0,1},{1,0},{2,3},{3,2},{4,5},{5,4},{6,7},{7,6},{8,9},{9,8},{10,11... | collective-permute-start | bytes 1572872 | tf_op jit(solution)/shard_map/ppermute | solution.py:208
  104.2 1.3 %collective-permute-start.3 = (f32[8,256]{1,0:T(8,128)S(1)}, f32[8,256]{1,0:T(8,128)S(1)}, u32[]{:S(2)}, u32[]{:S(2)}) collective-permute-start(f32[8,256]{1,0:T(8,128)S(1)} %shard_map.111.mine_ref), channel_id=1, source_target_pairs={{0,1},{1,0},{2,3},{3,2},{4,5},{5,4},{6,7},{7,6},{8,9},{9,8},{10,11... | collective-permute-start | bytes 24584 | tf_op jit(solution)/shard_map/ppermute | solution.py:208

commit v4 on v3

--- a/solution.py
+++ b/solution.py
@@ -42,12 +42,9 @@
     return (wide == lax.broadcasted_iota(jnp.int32, (count, slab), 1)).astype(BF16)
 
 
-def spread(values, hub_ref, slot_ref, out_ref):
+def spread(hub, slot, out_ref):
     peers, rows, width = out_ref.shape
-    hubs = hub_ref.shape[1]
-    slab = values.shape[0]
-    hub = dot(one_hot(hub_ref[...], slab), values)
-    slot = dot(one_hot(slot_ref[...], slab), values)
+    hubs = hub.shape[0]
     whole = jnp.concatenate(
         [
             jnp.broadcast_to(hub[None], (peers, hubs, width)),
@@ -63,9 +60,19 @@
     copies = [pltpu.make_async_copy(src, dst, sems.at[i]) for i, (src, dst) in enumerate(pairs)]
     for copy in copies:
         copy.start()
-    for copy in copies:
-        copy.wait()
-    spread(feat_ref[...], hub_ref, slot_ref, out_ref)
+    copies[0].wait()
+    copies[1].wait()
+    slab = feat_ref.shape[0]
+    hub_hot = one_hot(hub_ref[...], slab)
+    slot_hot = one_hot(slot_ref[...], slab)
+    copies[2].wait()
+    spread(dot(hub_hot, feat_ref[...]), dot(slot_hot, feat_ref[...]), out_ref)
+
+
+def pick_sum_body(part_ref, away_ref, hub_ref, slot_ref, out_ref):
+    values = (part_ref[...] + away_ref[...]).astype(BF16)
+    slab = values.shape[0]
+    spread(dot(one_hot(hub_ref[...], slab), values), dot(one_hot(slot_ref[...], slab), values), out_ref)
 
 
 def pick(packet, feats, hub_row, slot_row, flops):
@@ -79,10 +86,6 @@
         compiler_params=pltpu.CompilerParams(vmem_limit_bytes=16 * MIB),
         cost_estimate=pl.CostEstimate(flops=flops, bytes_accessed=0, transcendentals=0),
     )(*(pltpu.with_memory_space_constraint(x, pltpu.HBM) for x in (feats, hub_row, slot_row)))
-
-
-def pick_sum_body(part_ref, away_ref, hub_ref, slot_ref, out_ref):
-    spread((part_ref[...] + away_ref[...]).astype(BF16), hub_ref, slot_ref, out_ref)
 
 
 def split(got_ref, hubs):
@@ -139,39 +142,42 @@
     ).astype(BF16)
 
 
-def back_rows(hubs, step, start, dsec_ref, got_ref, w_ref, hub_mat, sparse_mat, acc_ref):
+def back_own_body(step, dsec_ref, hub_mat, sparse_mat, hub_out, slot_out):
     half = dsec_ref.shape[1]
+    src = pl.ds(pl.multiple_of(lax.axis_index("rep") * half, half), half)
+    slot_out[...] = dot(dsec_ref[...], sparse_mat[src, :])
+
+    @pl.loop(0, hub_mat.shape[1] // step)
+    def _(i):
+        at = pl.ds(pl.multiple_of(i * step, step), step)
+        hub_out[:, at] = dot(dsec_ref[...], hub_mat[src, at])
+
+
+def back_away_body(
+    hubs, step, hub_own, slot_own, grad_ref, dsec_ref, got_ref, w_ref, hub_mat, sparse_mat, out_ref, acc_ref
+):
+    half = dsec_ref.shape[1]
+    src = pl.ds(pl.multiple_of((1 - lax.axis_index("rep")) * half, half), half)
     peers, rows, width = got_ref.shape
     w_t = w_ref[...].astype(F32).T.astype(BF16)
-    src = pl.ds(pl.multiple_of(start, half), half)
-
-    def term(cols, mat):
+
+    def term(cols, mat, own):
         hid = dot_t(w_t, cols)
-        grad = jnp.where(hid > 0, dot(dsec_ref[...], mat), 0.0).astype(BF16)
+        grad = jnp.where(hid > 0, dot(dsec_ref[...], mat) + own, 0.0).astype(BF16)
         return dot(grad, cols)
 
     slot = got_ref[:, hubs:, :].astype(F32).reshape(peers * (rows - hubs), width).astype(BF16)
-    acc_ref[...] = term(slot, sparse_mat[src, :])
+    acc_ref[...] = term(slot, sparse_mat[src, :], slot_own[...])
     group = step // hubs
 
     @pl.loop(0, hub_mat.shape[1] // step)
     def _(i):
         at = pl.ds(pl.multiple_of(i * step, step), step)
         cols = got_ref[pl.ds(i * group, group), :hubs, :].reshape(step, width)
-        acc_ref[...] += term(cols, hub_mat[src, at])
-
-
-def back_own_body(hubs, step, dsec_ref, got_ref, w_ref, hub_mat, sparse_mat, acc_ref):
-    start = lax.axis_index("rep") * dsec_ref.shape[1]
-    back_rows(hubs, step, start, dsec_ref, got_ref, w_ref, hub_mat, sparse_mat, acc_ref)
-
-
-def back_away_body(hubs, step, own_ref, grad_ref, dsec_ref, got_ref, w_ref, hub_mat, sparse_mat, out_ref, acc_ref):
-    start = (1 - lax.axis_index("rep")) * dsec_ref.shape[1]
-    back_rows(hubs, step, start, dsec_ref, got_ref, w_ref, hub_mat, sparse_mat, acc_ref)
-    width = got_ref.shape[2]
+        acc_ref[...] += term(cols, hub_mat[src, at], hub_own[:, at])
+
     classes = grad_ref.shape[0]
-    out_ref[:width, :] = (acc_ref[...] + own_ref[...]).T
+    out_ref[:width, :] = acc_ref[...].T
     out_ref[width : width + classes, :] = grad_ref[...]
     rest = out_ref.shape[0] - width - classes
     out_ref[width + classes :, :] = jnp.zeros((rest, out_ref.shape[1]), F32)
@@ -182,7 +188,16 @@
 
 
 def share_body(mine_ref, away_ref, out_ref):
-    out_ref[...] = jnp.broadcast_to((mine_ref[...] + away_ref[...])[None], out_ref.shape)
+    mine = (mine_ref[...] + away_ref[...]).astype(BF16).astype(F32)
+    out_ref[...] = jnp.broadcast_to(mine[None], out_ref.shape).astype(BF16)
+
+
+def parts_body(got_ref, in_ref, out_ref):
+    peers, rows, width = got_ref.shape
+    whole = got_ref[...].astype(F32).reshape(peers * rows, width)
+    first, second = in_ref.shape[0], out_ref.shape[0]
+    in_ref[...] = whole[:first]
+    out_ref[...] = whole[first : first + second]
 
 
 def on_device(node_feats, w_in, w_out, labels, hub_rows, send_rows, adj_hub, adj_sparse):
@@ -231,21 +246,22 @@
         part, away, w_out.T, labels.reshape(1, half),
     )
     oth = swap(dsec)
-    own = call(
-        functools.partial(back_own_body, hubs, STEP3), shape((hid, width), F32), dsec, got, w_in, hub_mat, sparse_mat,
+    hub_own, slot_own = call(
+        functools.partial(back_own_body, STEP3), (shape((hid, hub_cols), F32), shape((hid, slot_cols), F32)),
+        dsec, hub_mat, sparse_mat,
         flops=products * hid // 2,
     )
     count = width + classes
     share = -(-count // (8 * nrows)) * 8
     flat = call(
         functools.partial(back_away_body, hubs, STEP3), shape((share * nrows, hid), F32),
-        own, grad_out, oth, got, w_in, hub_mat, sparse_mat,
+        hub_own, slot_own, grad_out, oth, got, w_in, hub_mat, sparse_mat,
         scratch=[pltpu.VMEM((hid, width), F32)], flops=products * hid // 2,
     )
     mine = call(sum_body, shape((share, hid), F32), exchange(flat.reshape(nrows, share, hid)))
-    whole = call(share_body, shape((nrows, share, hid), F32), mine, swap(mine))
-    whole = exchange(whole).reshape(nrows * share, hid)
-    return (logits.T, whole[:width], whole[width:count].T)
+    whole = exchange(call(share_body, shape((nrows, share, hid), BF16), mine, swap(mine)))
+    grad_in, grad_out = call(parts_body, (shape((width, hid), F32), shape((classes, hid), F32)), whole)
+    return (logits.T, grad_in, grad_out.T)
 
 
 def solution(mesh):

time: 125 us -> 121 us (0.968)
  blocking collectives: 93.6 us -> 90.8 us
  local copies, waits for them, and re-layouts: 1.38 us -> 0.04 us
    all_to_all x4, blocking collectives: 93.6 us -> 90.8 us  [exchange(): return lax.all_to_all(x, 'rows', split_axis=0, concat_axis=0, tiled=True)]
    pallas_call x9 -> x10, Pallas kernels: 22.4 us -> 21.8 us  [call(): pl.pallas_call(body, out_shape=outs, in_specs=[VM] * len(args), out_specs...]
  transfers between devices with their start and end apart: 4 -> 4, of which waited for: 2 -> 2; matrix products, arithmetic and copies ran while one was open for 0% -> 0% of each run, Pallas kernels for 6% -> 5%
where the time goes in v4:
time: 121 us; the launch traced here: 120 us
  blocking collectives  90.8 us (75%)
  Pallas kernels  24.2 us (20%)
  waiting for transfers between devices  3.83 us (3%)
    all_to_all x4, blocking collectives, exchange(): return lax.all_to_all(x, 'rows', split_axis=0, concat_axis=0, tiled=True)  90.8 us
    pallas_call x10, Pallas kernels, call(): pl.pallas_call(body, out_shape=outs, in_specs=[VM] * len(args), out_specs...  21.8 us
    ppermute x4, waiting for transfers between devices, swap(): return lax.ppermute(x, 'rep', SWAP)  3.83 us
  transfers between devices with their start and end apart: 4, of which 2 were waited for; matrix products, arithmetic and copies ran while one was open for 0% of the time, Pallas kernels for 5%

profile of v4, /device:TPU:0, one launch (start us, length us, event | category | flops | bytes accessed | tf_op | source)
XLA Modules:
  0.0 120.5 jit_solution(14522732708152853824)
XLA Ops:
  0.6 0.0 copy-start
  0.6 2.4 %shard_map.103 = bf16[64,72,128]{2,1,0:T(8,128)(2,1)S(1)} custom-call(bf16[2048,128]{1,0:T(8,128)(2,1)} %feat_hbm.1, s32[1,64]{1,0:T(1,128)} %bitcast.24, s32[1,512]{1,0:T(1,128)} %bitcast.22), custom_call_target="tpu_custom_call" | custom-call | flops 4831838208 | tf_op jit(solution)/shard_map/pallas_call | solution.py:79
  3.0 0.0 copy-start.1
  3.0 31.6 %all_to_all.20.got_ref = bf16[64,72,128]{2,1,0:T(8,128)(2,1)S(1)} all-to-all(bf16[64,72,128]{2,1,0:T(8,128)(2,1)S(1)} %shard_map.103), channel_id=1, replica_groups=mesh['rows'=64,'rep'=2] {'rows'}, dimensions={0} | all-to-all | bytes 2359296 | tf_op jit(solution)/shard_map/all_to_all | solution.py:220
  34.7 0.0 copy-done
  34.7 0.0 copy-done.1
  34.7 5.1 %shard_map.104.part_ref = f32[2048,128]{1,0:T(8,128)S(1)} custom-call(bf16[64,72,128]{2,1,0:T(8,128)(2,1)S(1)} %all_to_all.20.got_ref, bf16[2048,4096]{1,0:T(8,128)(2,1)S(1)} %bitcast.9, bf16[2048,512]{1,0:T(8,128)(2,1)S(1)} %bitcast.14), custom_call_target="tpu_custom_call" | custom-call | flops 4831838208 | tf_op jit(solution)/shard_map/pallas_call | solution.py:27
  39.8 0.0 copy-start.2
  39.8 0.1 collective-permute-start
  39.9 2.6 %collective-permute-done.away_ref = f32[2048,128]{1,0:T(8,128)S(1)} collective-permute-done((f32[2048,128]{1,0:T(8,128)S(1)}, f32[2048,128]{1,0:T(8,128)S(1)}, u32[]{:S(2)}, u32[]{:S(2)}) %collective-permute-start) | collective-permute-done | bytes 1048608 | tf_op jit(solution)/shard_map/ppermute | solution.py:223
  42.5 0.0 copy-done.5
  42.5 0.0 copy-done.6
  42.5 1.0 shard_map.105
  43.5 25.2 %all_to_all.21.got_ref = bf16[64,72,128]{2,1,0:T(8,128)(2,1)S(1)} all-to-all(bf16[64,72,128]{2,1,0:T(8,128)(2,1)S(1)} %shard_map.105), channel_id=1, replica_groups=mesh['rows'=64,'rep'=2] {'rows'}, dimensions={0} | all-to-all | bytes 2359296 | tf_op jit(solution)/shard_map/all_to_all | solution.py:220
  68.7 3.7 %shard_map.106 = (f32[1024,256]{1,0:T(8,128)S(1)}, bf16[4096,256]{1,0:T(8,128)(2,1)S(1)}, bf16[512,256]{1,0:T(8,128)(2,1)S(1)}) custom-call(bf16[64,72,128]{2,1,0:T(8,128)(2,1)S(1)} %all_to_all.21.got_ref, bf16[128,256]{1,0:T(8,128)(2,1)S(1)} %copy-done.2, bf16[2048,4096]{1,0:T(8,128)(2,1)S(1)} %bitcast.10, bf16[2048,512]{1,0:T(8,128)(2,1)S(1)} %bitcast.15), custom_call_target="tpu_custom_call" | custom-call | flops 2415919104 | tf_op jit(solution)/shard_map/pallas_call | solution.py:27
  72.3 0.3 collective-permute-start.1
  72.6 0.0 copy-start.3
  72.6 0.0 copy-start.4
  72.6 2.6 %shard_map.107.part_ref = f32[1024,256]{1,0:T(8,128)S(1)} custom-call(bf16[4096,256]{1,0:T(8,128)(2,1)S(1)} %get-tuple-element.13.hid_hub, bf16[512,256]{1,0:T(8,128)(2,1)S(1)} %get-tuple-element.14.hid_slot, bf16[2048,4096]{1,0:T(8,128)(2,1)S(1)} %bitcast.11, bf16[2048,512]{1,0:T(8,128)(2,1)S(1)} %bitcast.16), custom_call_target="tpu_custom_call" | custom-call | flops 2415919104 | tf_op jit(solution)/shard_map/pallas_call | solution.py:27
  75.2 0.0 collective-permute-done.1.away_ref
  75.3 0.0 copy-done.4
  75.3 1.2 shard_map.108
  76.5 0.5 collective-permute-start.2
  76.9 3.0 %shard_map.109 = (f32[256,4096]{1,0:T(8,128)S(1)}, f32[256,512]{1,0:T(8,128)S(1)}) custom-call(bf16[256,1024]{1,0:T(8,128)(2,1)S(1)} %get-tuple-element.17.dsec_ref, bf16[2048,4096]{1,0:T(8,128)(2,1)S(1)} %bitcast.12, bf16[2048,512]{1,0:T(8,128)(2,1)S(1)} %bitcast.17), custom_call_target="tpu_custom_call" | custom-call | flops 2415919104 | tf_op jit(solution)/shard_map/pallas_call | solution.py:27
  79.9 0.0 collective-permute-done.2.dsec_ref
  79.9 4.6 %shard_map.110 = f32[512,256]{1,0:T(8,128)S(1)} custom-call(f32[256,4096]{1,0:T(8,128)S(1)} %get-tuple-element.18.hub_own, f32[256,512]{1,0:T(8,128)S(1)} %get-tuple-element.19.slot_own, f32[172,256]{1,0:T(8,128)S(1)} %get-tuple-element.20.grad_ref, bf16[256,1024]{1,0:T(8,128)(2,1)S(1)} %collective-permute-done.2.dsec_ref, ...), custom_call_target="tpu_custom_call" | custom-call | flops 2415919104 | tf_op jit(solution)/shard_map/pallas_call | solution.py:27
  84.5 18.4 %all_to_all.22.got_ref = f32[64,8,256]{2,1,0:T(8,128)S(1)} all-to-all(f32[64,8,256]{2,1,0:T(8,128)S(1)} %bitcast.19), channel_id=1, replica_groups=mesh['rows'=64,'rep'=2] {'rows'}, dimensions={0} | all-to-all | bytes 1048576 | tf_op jit(solution)/shard_map/all_to_all | solution.py:220
  102.9 0.1 shard_map.111.mine_ref
  103.0 0.1 collective-permute-start.3
  103.1 1.2 collective-permute-done.3.away_ref
  104.3 15.5 %all_to_all.23.got_ref = bf16[64,8,256]{2,1,0:T(8,128)(2,1)S(1)} all-to-all(bf16[64,8,256]{2,1,0:T(8,128)(2,1)S(1)} %shard_map.112), channel_id=1, replica_groups=mesh['rows'=64,'rep'=2] {'rows'}, dimensions={0} | all-to-all | bytes 524288 | tf_op jit(solution)/shard_map/all_to_all | solution.py:220
  119.8 0.7 shard_map.113
  (5 shorter events, 0.0 us)
Async XLA Ops:
  0.6 34.0 %copy-start = (bf16[2048,1,4096]{2,0,1:T(8,128)(2,1)S(1)}, bf16[2048,1,4096]{2,0,1:T(8,128)(2,1)}, u32[]{:S(2)}) copy-start(bf16[2048,1,4096]{2,0,1:T(8,128)(2,1)} %param.14) | copy-start | bytes 50331652
  3.0 31.7 %copy-start.1 = (bf16[2048,1,512]{2,0,1:T(8,128)(2,1)S(1)}, bf16[2048,1,512]{2,0,1:T(8,128)(2,1)}, u32[]{:S(2)}) copy-start(bf16[2048,1,512]{2,0,1:T(8,128)(2,1)} %param.15) | copy-start | bytes 6291460
  34.7 7.8 %copy-start.5 = (s32[1,1,512]{2,1,0:T(1,128)S(1)}, s32[1,1,512]{2,1,0:T(1,128)}, u32[]{:S(2)}) copy-start(s32[1,1,512]{2,1,0:T(1,128)} %param.13) | copy-start | bytes 6148
  34.7 7.8 %copy-start.6 = (s32[1,1,64]{2,1,0:T(1,128)S(1)}, s32[1,1,64]{2,1,0:T(1,128)}, u32[]{:S(2)}) copy-start(s32[1,1,64]{2,1,0:T(1,128)} %param.12) | copy-start | bytes 772
  39.8 28.9 %copy-start.2 = (bf16[128,256]{1,0:T(8,128)(2,1)S(1)}, bf16[128,256]{1,0:T(8,128)(2,1)}, u32[]{:S(2)}) copy-start(bf16[128,256]{1,0:T(8,128)(2,1)} %w_ref.3) | copy-start | bytes 196612
  39.8 2.7 %collective-permute-start = (f32[2048,128]{1,0:T(8,128)S(1)}, f32[2048,128]{1,0:T(8,128)S(1)}, u32[]{:S(2)}, u32[]{:S(2)}) collective-permute-start(f32[2048,128]{1,0:T(8,128)S(1)} %shard_map.104.part_ref), channel_id=1, source_target_pairs={{0,1},{1,0},{2,3},{3,2},{4,5},{5,4},{6,7},{7,6},{8,9},{9,8},{10,11... | collective-permute-start | bytes 3145736 | tf_op jit(solution)/shard_map/ppermute | solution.py:223
  72.3 2.9 %collective-permute-start.1 = (f32[1024,256]{1,0:T(8,128)S(1)}, f32[1024,256]{1,0:T(8,128)S(1)}, u32[]{:S(2)}, u32[]{:S(2)}) collective-permute-start(f32[1024,256]{1,0:T(8,128)S(1)} %get-tuple-element.15), channel_id=1, source_target_pairs={{0,1},{1,0},{2,3},{3,2},{4,5},{5,4},{6,7},{7,6},{8,9},{9,8},{10,11... | collective-permute-start | bytes 3145736 | tf_op jit(solution)/shard_map/ppermute | solution.py:223
  72.6 2.6 %copy-start.3 = (bf16[256,172]{0,1:T(8,128)(2,1)S(1)}, bf16[256,172]{0,1:T(8,128)(2,1)}, u32[]{:S(2)}) copy-start(bf16[256,172]{0,1:T(8,128)(2,1)} %param.10) | copy-start | bytes 264196
  72.6 2.6 %copy-start.4 = (s32[1024]{0:T(1024)S(1)}, s32[1024]{0:T(1024)}, u32[]{:S(2)}) copy-start(s32[1024]{0:T(1024)} %param.11) | copy-start | bytes 12292
  76.5 3.5 %collective-permute-start.2 = (bf16[256,1024]{1,0:T(8,128)(2,1)S(1)}, bf16[256,1024]{1,0:T(8,128)(2,1)S(1)}, u32[]{:S(2)}, u32[]{:S(2)}) collective-permute-start(bf16[256,1024]{1,0:T(8,128)(2,1)S(1)} %get-tuple-element.17.dsec_ref), channel_id=1, source_target_pairs={{0,1},{1,0},{2,3},{3,2},{4,5},{5,4},{6,7},{7,6},{8,9},{9,8},{10,11... | collective-permute-start | bytes 1572872 | tf_op jit(solution)/shard_map/ppermute | solution.py:223
  103.0 1.3 %collective-permute-start.3 = (f32[8,256]{1,0:T(8,128)S(1)}, f32[8,256]{1,0:T(8,128)S(1)}, u32[]{:S(2)}, u32[]{:S(2)}) collective-permute-start(f32[8,256]{1,0:T(8,128)S(1)} %shard_map.111.mine_ref), channel_id=1, source_target_pairs={{0,1},{1,0},{2,3},{3,2},{4,5},{5,4},{6,7},{7,6},{8,9},{9,8},{10,11... | collective-permute-start | bytes 24584 | tf_op jit(solution)/shard_map/ppermute | solution.py:223

commit v5 on v4

--- a/solution.py
+++ b/solution.py
@@ -10,9 +10,12 @@
 F32, BF16 = jnp.float32, jnp.bfloat16
 VM = pl.BlockSpec(memory_space=pltpu.VMEM)
 MIB = 1024 * 1024
-STEP1 = 2048
-STEP2 = 1024
-STEP3 = 2048
+PIECES = 1
+TOP = 6
+STEP1 = 1024
+STEP2 = 512
+STEP3 = 4096
+STEP4 = 4096
 
 
 def dot(a, b):
@@ -55,37 +58,59 @@
     out_ref[...] = whole.astype(BF16)
 
 
-def pick_body(feat_hbm, hub_hbm, slot_hbm, out_ref, feat_ref, hub_ref, slot_ref, sems):
-    pairs = ((hub_hbm, hub_ref), (slot_hbm, slot_ref), (feat_hbm, feat_ref))
-    copies = [pltpu.make_async_copy(src, dst, sems.at[i]) for i, (src, dst) in enumerate(pairs)]
+def pick_body(feat_hbm, hub_hbm, slot_hbm, out_ref, hub_hot, slot_hot, feat_ref, hub_ref, slot_ref, sems):
+    slab = feat_ref.shape[0]
+    rows = slab // PIECES
+    copies = [
+        pltpu.make_async_copy(hub_hbm, hub_ref, sems.at[PIECES]),
+        pltpu.make_async_copy(slot_hbm, slot_ref, sems.at[PIECES + 1]),
+    ]
+    for i in range(PIECES):
+        at = pl.ds(i * rows, rows)
+        copies.append(pltpu.make_async_copy(feat_hbm.at[at], feat_ref.at[at], sems.at[i]))
     for copy in copies:
         copy.start()
     copies[0].wait()
     copies[1].wait()
-    slab = feat_ref.shape[0]
-    hub_hot = one_hot(hub_ref[...], slab)
-    slot_hot = one_hot(slot_ref[...], slab)
-    copies[2].wait()
-    spread(dot(hub_hot, feat_ref[...]), dot(slot_hot, feat_ref[...]), out_ref)
-
-
-def pick_sum_body(part_ref, away_ref, hub_ref, slot_ref, out_ref):
-    values = (part_ref[...] + away_ref[...]).astype(BF16)
-    slab = values.shape[0]
-    spread(dot(one_hot(hub_ref[...], slab), values), dot(one_hot(slot_ref[...], slab), values), out_ref)
+    hub_hot[...] = one_hot(hub_ref[...], slab)
+    slot_hot[...] = one_hot(slot_ref[...], slab)
+    hub = slot = 0.0
+    for i in range(PIECES):
+        at = pl.ds(i * rows, rows)
+        copies[2 + i].wait()
+        hub += dot(hub_hot[:, at], feat_ref[at, :])
+        slot += dot(slot_hot[:, at], feat_ref[at, :])
+    spread(hub, slot, out_ref)
 
 
 def pick(packet, feats, hub_row, slot_row, flops):
     return pl.pallas_call(
         pick_body,
-        out_shape=packet,
+        out_shape=(packet,)
+        + tuple(jax.ShapeDtypeStruct((x.shape[1], feats.shape[0]), BF16) for x in (hub_row, slot_row)),
         in_specs=[pl.BlockSpec(memory_space=pl.ANY)] * 3,
-        out_specs=VM,
+        out_specs=(VM, VM, VM),
         scratch_shapes=[pltpu.VMEM(x.shape, x.dtype) for x in (feats, hub_row, slot_row)]
-        + [pltpu.SemaphoreType.DMA((3,))],
+        + [pltpu.SemaphoreType.DMA((PIECES + 2,))],
         compiler_params=pltpu.CompilerParams(vmem_limit_bytes=16 * MIB),
         cost_estimate=pl.CostEstimate(flops=flops, bytes_accessed=0, transcendentals=0),
     )(*(pltpu.with_memory_space_constraint(x, pltpu.HBM) for x in (feats, hub_row, slot_row)))
+
+
+def pick_top_body(part_ref, away_ref, hub_hot, slot_hot, hub_ref, slot_ref):
+    values = (part_ref[...] + away_ref[...]).astype(BF16)
+    top = pl.ds(0, values.shape[0])
+    hub_ref[...] = dot(hub_hot[:, top], values)
+    slot_ref[...] = dot(slot_hot[:, top], values)
+
+
+def pick_rest_body(part_ref, away_ref, hub_hot, slot_hot, hub_ref, slot_ref, out_ref):
+    values = (part_ref[...] + away_ref[...]).astype(BF16)
+    count = values.shape[0]
+    rest = pl.ds(hub_hot.shape[1] - count, count)
+    hub = hub_ref[...] + dot(hub_hot[:, rest], values)
+    slot = slot_ref[...] + dot(slot_hot[:, rest], values)
+    spread(hub, slot, out_ref)
 
 
 def split(got_ref, hubs):
@@ -95,13 +120,10 @@
     return hub, slot
 
 
-def first_body(hubs, step, got_ref, hub_mat, sparse_mat, part_ref):
+def first_body(hubs, start, got_ref, hub_mat, sparse_mat, part_ref):
     hub, slot = split(got_ref, hubs)
-
-    @pl.loop(0, part_ref.shape[0] // step)
-    def _(i):
-        at = pl.ds(pl.multiple_of(i * step, step), step)
-        part_ref[at, :] = dot(hub_mat[at, :], hub) + dot(sparse_mat[at, :], slot)
+    at = pl.ds(start, part_ref.shape[0])
+    part_ref[...] = dot(hub_mat[at, :], hub) + dot(sparse_mat[at, :], slot)
 
 
 def second_rows(step, start, part_ref, hid_hub, hid_slot, hub_mat, sparse_mat):
@@ -177,14 +199,13 @@
         acc_ref[...] += term(cols, hub_mat[src, at], hub_own[:, at])
 
     classes = grad_ref.shape[0]
-    out_ref[:width, :] = acc_ref[...].T
-    out_ref[width : width + classes, :] = grad_ref[...]
-    rest = out_ref.shape[0] - width - classes
-    out_ref[width + classes :, :] = jnp.zeros((rest, out_ref.shape[1]), F32)
+    rest = out_ref.shape[0] * out_ref.shape[1] - width - classes
+    flat = jnp.concatenate([acc_ref[...].T, grad_ref[...], jnp.zeros((rest, out_ref.shape[2]), F32)], axis=0)
+    out_ref[...] = flat.reshape(out_ref.shape).astype(BF16)
 
 
 def sum_body(got_ref, out_ref):
-    out_ref[...] = jnp.sum(got_ref[...], axis=0)
+    out_ref[...] = jnp.sum(got_ref[...].astype(F32), axis=0)
 
 
 def share_body(mine_ref, away_ref, out_ref):
@@ -222,12 +243,25 @@
     def swap(x):
         return lax.ppermute(x, "rep", SWAP)
 
-    got = exchange(pick(packet, node_feats, hub_row, slot_row, products * 256))
-    part = call(
-        functools.partial(first_body, hubs, STEP1), shape((slab, width), F32), got, hub_mat, sparse_mat,
-        flops=products * width * 2,
-    )
-    got = exchange(call(pick_sum_body, packet, part, swap(part), hub_row, slot_row))
+    sent, hub_hot, slot_hot = pick(packet, node_feats, hub_row, slot_row, products * 256)
+    got = exchange(sent)
+
+    def first_rows(start, rows):
+        return call(
+            functools.partial(first_body, hubs, start), shape((rows, width), F32), got, hub_mat, sparse_mat,
+            flops=products * rows // slab * width * 2,
+        )
+
+    top = slab * TOP // 8
+    part = first_rows(0, top)
+    away = swap(part)
+    part_rest = first_rows(top, slab - top)
+    away_rest = swap(part_rest)
+    hub_some, slot_some = call(
+        pick_top_body, (shape((hubs, width), F32), shape((slot_cols, width), F32)), part, away, hub_hot, slot_hot,
+        flops=2 * (hubs + slot_cols) * slab * width,
+    )
+    got = exchange(call(pick_rest_body, packet, part_rest, away_rest, hub_hot, slot_hot, hub_some, slot_some))
     part, hid_hub, hid_slot = call(
         functools.partial(away_body, hubs, STEP2),
         (shape((half, hid), F32), shape((hub_cols, hid), BF16), shape((slot_cols, hid), BF16)),
@@ -236,7 +270,7 @@
     )
     away = swap(part)
     part = call(
-        functools.partial(own_body, STEP2), shape((half, hid), F32), hid_hub, hid_slot, hub_mat, sparse_mat,
+        functools.partial(own_body, STEP1), shape((half, hid), F32), hid_hub, hid_slot, hub_mat, sparse_mat,
         flops=products * hid // 2,
     )
     scale = float(1.0 / (slab * nrows) ** 0.5)
@@ -254,11 +288,11 @@
     count = width + classes
     share = -(-count // (8 * nrows)) * 8
     flat = call(
-        functools.partial(back_away_body, hubs, STEP3), shape((share * nrows, hid), F32),
+        functools.partial(back_away_body, hubs, STEP4), shape((nrows, share, hid), BF16),
         hub_own, slot_own, grad_out, oth, got, w_in, hub_mat, sparse_mat,
         scratch=[pltpu.VMEM((hid, width), F32)], flops=products * hid // 2,
     )
-    mine = call(sum_body, shape((share, hid), F32), exchange(flat.reshape(nrows, share, hid)))
+    mine = call(sum_body, shape((share, hid), F32), exchange(flat))
     whole = exchange(call(share_body, shape((nrows, share, hid), BF16), mine, swap(mine)))
     grad_in, grad_out = call(parts_body, (shape((width, hid), F32), shape((classes, hid), F32)), whole)
     return (logits.T, grad_in, grad_out.T)

time: 121 us -> 116 us (0.959)
  blocking collectives: 90.8 us -> 88.4 us
  waiting for transfers between devices: 3.83 us -> 1.66 us
    all_to_all x4, blocking collectives: 90.8 us -> 88.4 us  [exchange(): return lax.all_to_all(x, 'rows', split_axis=0, concat_axis=0, tiled=True)]
    ppermute x4 -> x5, waiting for transfers between devices: 3.83 us -> 1.66 us  [swap(): return lax.ppermute(x, 'rep', SWAP)]
    pallas_call x10 -> x12, Pallas kernels: 21.8 us -> 21.1 us  [call(): pl.pallas_call(body, out_shape=outs, in_specs=[VM] * len(args), out_specs...]
  transfers between devices with their start and end apart: 4 -> 5, of which waited for: 2 -> 3; matrix products, arithmetic and copies ran while one was open for 0% -> 0% of each run, Pallas kernels for 5% -> 6%
where the time goes in v5:
time: 116 us
  blocking collectives  88.4 us (76%)
  Pallas kernels  23.2 us (20%)
  waiting for transfers between devices  1.66 us (1%)
  starting transfers between devices  1.48 us (1%)
    all_to_all x4, blocking collectives, exchange(): return lax.all_to_all(x, 'rows', split_axis=0, concat_axis=0, tiled=True)  88.4 us
    pallas_call x12, Pallas kernels, call(): pl.pallas_call(body, out_shape=outs, in_specs=[VM] * len(args), out_specs...  21.1 us
  transfers between devices with their start and end apart: 5, of which 3 were waited for; matrix products, arithmetic and copies ran while one was open for 0% of the time, Pallas kernels for 6%

profile of v5, /device:TPU:0, one launch (start us, length us, event | category | flops | bytes accessed | tf_op | source)
XLA Modules:
  0.0 115.6 jit_solution(17131491701617786930)
XLA Ops:
  0.6 2.1 %shard_map.103 = (bf16[64,72,128]{2,1,0:T(8,128)(2,1)S(1)}, bf16[64,2048]{1,0:T(8,128)(2,1)S(1)}, bf16[512,2048]{1,0:T(8,128)(2,1)S(1)}) custom-call(bf16[2048,128]{1,0:T(8,128)(2,1)} %feat_hbm.1, s32[1,64]{1,0:T(1,128)} %bitcast.25, s32[1,512]{1,0:T(1,128)} %bitcast.24), custom_call_target="tpu_custom_call" | custom-call | flops 4831838208 | tf_op jit(solution)/shard_map/pallas_call | solution.py:87
  2.8 0.0 copy-start.1
  2.8 31.6 %all_to_all.20.got_ref = bf16[64,72,128]{2,1,0:T(8,128)(2,1)S(1)} all-to-all(bf16[64,72,128]{2,1,0:T(8,128)(2,1)S(1)} %get-tuple-element.18), channel_id=1, replica_groups=mesh['rows'=64,'rep'=2] {'rows'}, dimensions={0} | all-to-all | bytes 2359296 | tf_op jit(solution)/shard_map/all_to_all | solution.py:241
  34.4 0.0 copy-done
  34.4 3.8 %shard_map.105.part_ref = f32[1536,128]{1,0:T(8,128)S(1)} custom-call(bf16[64,72,128]{2,1,0:T(8,128)(2,1)S(1)} %all_to_all.20.got_ref, bf16[2048,4096]{1,0:T(8,128)(2,1)S(1)} %bitcast.8, bf16[2048,512]{1,0:T(8,128)(2,1)S(1)} %bitcast.14), custom_call_target="tpu_custom_call" | custom-call | flops 3623878656 | tf_op jit(solution)/shard_map/pallas_call | solution.py:30
  38.3 0.1 collective-permute-start.1
  38.4 1.4 %shard_map.104.part_ref = f32[512,128]{1,0:T(8,128)S(1)} custom-call(bf16[64,72,128]{2,1,0:T(8,128)(2,1)S(1)} %all_to_all.20.got_ref, bf16[2048,4096]{1,0:T(8,128)(2,1)S(1)} %bitcast.9, bf16[2048,512]{1,0:T(8,128)(2,1)S(1)} %bitcast.15), custom_call_target="tpu_custom_call" | custom-call | flops 1207959552 | tf_op jit(solution)/shard_map/pallas_call | solution.py:30
  39.8 0.6 collective-permute-start
  40.3 0.3 collective-permute-done.1.away_ref
  40.7 0.7 shard_map.106
  41.3 0.2 collective-permute-done.away_ref
  41.5 0.3 shard_map.107
  41.9 0.0 copy-start.2
  41.9 25.6 %all_to_all.21.got_ref = bf16[64,72,128]{2,1,0:T(8,128)(2,1)S(1)} all-to-all(bf16[64,72,128]{2,1,0:T(8,128)(2,1)S(1)} %shard_map.107), channel_id=1, replica_groups=mesh['rows'=64,'rep'=2] {'rows'}, dimensions={0} | all-to-all | bytes 2359296 | tf_op jit(solution)/shard_map/all_to_all | solution.py:241
  67.5 3.5 %shard_map.108 = (f32[1024,256]{1,0:T(8,128)S(1)}, bf16[4096,256]{1,0:T(8,128)(2,1)S(1)}, bf16[512,256]{1,0:T(8,128)(2,1)S(1)}) custom-call(bf16[64,72,128]{2,1,0:T(8,128)(2,1)S(1)} %all_to_all.21.got_ref, bf16[128,256]{1,0:T(8,128)(2,1)S(1)} %copy-done.2, bf16[2048,4096]{1,0:T(8,128)(2,1)S(1)} %bitcast.10, bf16[2048,512]{1,0:T(8,128)(2,1)S(1)} %bitcast.16), custom_call_target="tpu_custom_call" | custom-call | flops 2415919104 | tf_op jit(solution)/shard_map/pallas_call | solution.py:30
  71.0 0.3 collective-permute-start.2
  71.3 0.0 copy-start.3
  71.3 0.0 copy-start.4
  71.3 2.6 %shard_map.109.part_ref = f32[1024,256]{1,0:T(8,128)S(1)} custom-call(bf16[4096,256]{1,0:T(8,128)(2,1)S(1)} %get-tuple-element.23.hid_hub, bf16[512,256]{1,0:T(8,128)(2,1)S(1)} %get-tuple-element.24.hid_slot, bf16[2048,4096]{1,0:T(8,128)(2,1)S(1)} %bitcast.11, bf16[2048,512]{1,0:T(8,128)(2,1)S(1)} %bitcast.17), custom_call_target="tpu_custom_call" | custom-call | flops 2415919104 | tf_op jit(solution)/shard_map/pallas_call | solution.py:30
  73.9 0.0 collective-permute-done.2.away_ref
  73.9 0.0 copy-done.4
  73.9 1.2 %shard_map.110 = (bf16[172,1024]{1,0:T(8,128)(2,1)}, bf16[256,1024]{1,0:T(8,128)(2,1)S(1)}, f32[172,256]{1,0:T(8,128)S(1)}) custom-call(f32[1024,256]{1,0:T(8,128)S(1)} %shard_map.109.part_ref, f32[1024,256]{1,0:T(8,128)S(1)} %collective-permute-done.2.away_ref, bf16[172,256]{1,0:T(8,128)(2,1)S(1)} %bitcast.20, s32[1,1024]{1,0:T(1,128)S(1)} %bitcast.21), custom_call_target="tpu_custom_call" | custom-call | tf_op jit(solution)/shard_map/pallas_call | solution.py:30
  75.1 0.5 collective-permute-start.3
  75.6 2.6 %shard_map.111 = (f32[256,4096]{1,0:T(8,128)S(1)}, f32[256,512]{1,0:T(8,128)S(1)}) custom-call(bf16[256,1024]{1,0:T(8,128)(2,1)S(1)} %get-tuple-element.27.dsec_ref, bf16[2048,4096]{1,0:T(8,128)(2,1)S(1)} %bitcast.12, bf16[2048,512]{1,0:T(8,128)(2,1)S(1)} %bitcast.18), custom_call_target="tpu_custom_call" | custom-call | flops 2415919104 | tf_op jit(solution)/shard_map/pallas_call | solution.py:30
  78.2 0.0 collective-permute-done.3.dsec_ref
  78.2 4.1 %shard_map.112 = bf16[64,8,256]{2,1,0:T(8,128)(2,1)S(1)} custom-call(f32[256,4096]{1,0:T(8,128)S(1)} %get-tuple-element.28.hub_own, f32[256,512]{1,0:T(8,128)S(1)} %get-tuple-element.29.slot_own, f32[172,256]{1,0:T(8,128)S(1)} %get-tuple-element.30.grad_ref, bf16[256,1024]{1,0:T(8,128)(2,1)S(1)} %collective-permute-done.3.dsec_ref, ...), custom_call_target="tpu_custom_call" | custom-call | flops 2415919104 | tf_op jit(solution)/shard_map/pallas_call | solution.py:30
  82.3 15.6 %all_to_all.22.got_ref = bf16[64,8,256]{2,1,0:T(8,128)(2,1)S(1)} all-to-all(bf16[64,8,256]{2,1,0:T(8,128)(2,1)S(1)} %shard_map.112), channel_id=1, replica_groups=mesh['rows'=64,'rep'=2] {'rows'}, dimensions={0} | all-to-all | bytes 524288 | tf_op jit(solution)/shard_map/all_to_all | solution.py:241
  97.9 0.1 shard_map.113.mine_ref
  98.0 0.1 collective-permute-start.4
  98.1 1.2 %collective-permute-done.4.away_ref = f32[8,256]{1,0:T(8,128)S(1)} collective-permute-done((f32[8,256]{1,0:T(8,128)S(1)}, f32[8,256]{1,0:T(8,128)S(1)}, u32[]{:S(2)}, u32[]{:S(2)}) %collective-permute-start.4) | collective-permute-done | bytes 8224 | tf_op jit(solution)/shard_map/ppermute | solution.py:244
  99.3 15.6 %all_to_all.23.got_ref = bf16[64,8,256]{2,1,0:T(8,128)(2,1)S(1)} all-to-all(bf16[64,8,256]{2,1,0:T(8,128)(2,1)S(1)} %shard_map.114), channel_id=1, replica_groups=mesh['rows'=64,'rep'=2] {'rows'}, dimensions={0} | all-to-all | bytes 524288 | tf_op jit(solution)/shard_map/all_to_all | solution.py:241
  114.9 0.7 shard_map.115
  (5 shorter events, 0.0 us)
Async XLA Ops:
  0.6 33.8 %copy-start = (bf16[2048,1,4096]{2,0,1:T(8,128)(2,1)S(1)}, bf16[2048,1,4096]{2,0,1:T(8,128)(2,1)}, u32[]{:S(2)}) copy-start(bf16[2048,1,4096]{2,0,1:T(8,128)(2,1)} %param.14) | copy-start | bytes 50331652
  2.8 31.7 %copy-start.1 = (bf16[2048,1,512]{2,0,1:T(8,128)(2,1)S(1)}, bf16[2048,1,512]{2,0,1:T(8,128)(2,1)}, u32[]{:S(2)}) copy-start(bf16[2048,1,512]{2,0,1:T(8,128)(2,1)} %param.15) | copy-start | bytes 6291460
  38.3 2.4 %collective-permute-start.1 = (f32[1536,128]{1,0:T(8,128)S(1)}, f32[1536,128]{1,0:T(8,128)S(1)}, u32[]{:S(2)}, u32[]{:S(2)}) collective-permute-start(f32[1536,128]{1,0:T(8,128)S(1)} %shard_map.105.part_ref), channel_id=1, source_target_pairs={{0,1},{1,0},{2,3},{3,2},{4,5},{5,4},{6,7},{7,6},{8,9},{9,8},{10,11... | collective-permute-start | bytes 2359304 | tf_op jit(solution)/shard_map/ppermute | solution.py:244
  39.8 1.7 %collective-permute-start = (f32[512,128]{1,0:T(8,128)S(1)}, f32[512,128]{1,0:T(8,128)S(1)}, u32[]{:S(2)}, u32[]{:S(2)}) collective-permute-start(f32[512,128]{1,0:T(8,128)S(1)} %shard_map.104.part_ref), channel_id=1, source_target_pairs={{0,1},{1,0},{2,3},{3,2},{4,5},{5,4},{6,7},{7,6},{8,9},{9,8},{10,11... | collective-permute-start | bytes 786440 | tf_op jit(solution)/shard_map/ppermute | solution.py:244
  41.9 25.6 %copy-start.2 = (bf16[128,256]{1,0:T(8,128)(2,1)S(1)}, bf16[128,256]{1,0:T(8,128)(2,1)}, u32[]{:S(2)}) copy-start(bf16[128,256]{1,0:T(8,128)(2,1)} %w_ref.3) | copy-start | bytes 196612
  71.0 2.9 %collective-permute-start.2 = (f32[1024,256]{1,0:T(8,128)S(1)}, f32[1024,256]{1,0:T(8,128)S(1)}, u32[]{:S(2)}, u32[]{:S(2)}) collective-permute-start(f32[1024,256]{1,0:T(8,128)S(1)} %get-tuple-element.25), channel_id=1, source_target_pairs={{0,1},{1,0},{2,3},{3,2},{4,5},{5,4},{6,7},{7,6},{8,9},{9,8},{10,11... | collective-permute-start | bytes 3145736 | tf_op jit(solution)/shard_map/ppermute | solution.py:244
  71.3 2.6 %copy-start.3 = (bf16[256,172]{0,1:T(8,128)(2,1)S(1)}, bf16[256,172]{0,1:T(8,128)(2,1)}, u32[]{:S(2)}) copy-start(bf16[256,172]{0,1:T(8,128)(2,1)} %param.10) | copy-start | bytes 264196
  71.3 2.6 %copy-start.4 = (s32[1024]{0:T(1024)S(1)}, s32[1024]{0:T(1024)}, u32[]{:S(2)}) copy-start(s32[1024]{0:T(1024)} %param.11) | copy-start | bytes 12292
  75.1 3.1 %collective-permute-start.3 = (bf16[256,1024]{1,0:T(8,128)(2,1)S(1)}, bf16[256,1024]{1,0:T(8,128)(2,1)S(1)}, u32[]{:S(2)}, u32[]{:S(2)}) collective-permute-start(bf16[256,1024]{1,0:T(8,128)(2,1)S(1)} %get-tuple-element.27.dsec_ref), channel_id=1, source_target_pairs={{0,1},{1,0},{2,3},{3,2},{4,5},{5,4},{6,7},{7,6},{8,9},{9,8},{10,11... | collective-permute-start | bytes 1572872 | tf_op jit(solution)/shard_map/ppermute | solution.py:244
  98.0 1.2 %collective-permute-start.4 = (f32[8,256]{1,0:T(8,128)S(1)}, f32[8,256]{1,0:T(8,128)S(1)}, u32[]{:S(2)}, u32[]{:S(2)}) collective-permute-start(f32[8,256]{1,0:T(8,128)S(1)} %shard_map.113.mine_ref), channel_id=1, source_target_pairs={{0,1},{1,0},{2,3},{3,2},{4,5},{5,4},{6,7},{7,6},{8,9},{9,8},{10,11... | collective-permute-start | bytes 24584 | tf_op jit(solution)/shard_map/ppermute | solution.py:244

commit v6 on v5

--- a/solution.py
+++ b/solution.py
@@ -15,7 +15,7 @@
 STEP1 = 1024
 STEP2 = 512
 STEP3 = 4096
-STEP4 = 4096
+STEP4 = 2048
 
 
 def dot(a, b):
@@ -127,9 +127,8 @@
 
 
 def second_rows(step, start, part_ref, hid_hub, hid_slot, hub_mat, sparse_mat):
-    @pl.loop(0, part_ref.shape[0] // step)
-    def _(i):
-        at = pl.ds(pl.multiple_of(i * step, step), step)
+    for i in range(part_ref.shape[0] // step):
+        at = pl.ds(i * step, step)
         src = pl.ds(pl.multiple_of(start + i * step, step), step)
         part_ref[at, :] = dot(hub_mat[src, :], hid_hub[...]) + dot(sparse_mat[src, :], hid_slot[...])
 
@@ -176,27 +175,26 @@
 
 
 def back_away_body(
-    hubs, step, hub_own, slot_own, grad_ref, dsec_ref, got_ref, w_ref, hub_mat, sparse_mat, out_ref, acc_ref
+    hubs, step, hub_own, slot_own, grad_ref, dsec_ref, got_ref, hid_hub, hid_slot, hub_mat, sparse_mat, out_ref, acc_ref
 ):
     half = dsec_ref.shape[1]
     src = pl.ds(pl.multiple_of((1 - lax.axis_index("rep")) * half, half), half)
     peers, rows, width = got_ref.shape
-    w_t = w_ref[...].astype(F32).T.astype(BF16)
-
-    def term(cols, mat, own):
-        hid = dot_t(w_t, cols)
-        grad = jnp.where(hid > 0, dot(dsec_ref[...], mat) + own, 0.0).astype(BF16)
+
+    def term(cols, mat, own, hid):
+        grad = jnp.where(hid.astype(F32).T > 0, dot(dsec_ref[...], mat) + own, 0.0).astype(BF16)
         return dot(grad, cols)
 
     slot = got_ref[:, hubs:, :].astype(F32).reshape(peers * (rows - hubs), width).astype(BF16)
-    acc_ref[...] = term(slot, sparse_mat[src, :], slot_own[...])
+    acc_ref[...] = term(slot, sparse_mat[src, :], slot_own[...], hid_slot[...])
     group = step // hubs
 
-    @pl.loop(0, hub_mat.shape[1] // step)
-    def _(i):
-        at = pl.ds(pl.multiple_of(i * step, step), step)
+    total = 0.0
+    for i in range(hub_mat.shape[1] // step):
+        at = pl.ds(i * step, step)
         cols = got_ref[pl.ds(i * group, group), :hubs, :].reshape(step, width)
-        acc_ref[...] += term(cols, hub_mat[src, at], hub_own[:, at])
+        total += term(cols, hub_mat[src, at], hub_own[:, at], hid_hub[at, :])
+    acc_ref[...] += total
 
     classes = grad_ref.shape[0]
     rest = out_ref.shape[0] * out_ref.shape[1] - width - classes
@@ -289,7 +287,7 @@
     share = -(-count // (8 * nrows)) * 8
     flat = call(
         functools.partial(back_away_body, hubs, STEP4), shape((nrows, share, hid), BF16),
-        hub_own, slot_own, grad_out, oth, got, w_in, hub_mat, sparse_mat,
+        hub_own, slot_own, grad_out, oth, got, hid_hub, hid_slot, hub_mat, sparse_mat,
         scratch=[pltpu.VMEM((hid, width), F32)], flops=products * hid // 2,
     )
     mine = call(sum_body, shape((share, hid), F32), exchange(flat))

time: 116 us -> 115 us (level)
  no operation moved by 1% of the time
where the time goes in v6:
time: 115 us
  blocking collectives  88.4 us (77%)
  Pallas kernels  22.4 us (19%)
  waiting for transfers between devices  1.65 us (1%)
  starting transfers between devices  1.48 us (1%)
    all_to_all x4, blocking collectives, exchange(): return lax.all_to_all(x, 'rows', split_axis=0, concat_axis=0, tiled=True)  88.4 us
    pallas_call x12, Pallas kernels, call(): pl.pallas_call(body, out_shape=outs, in_specs=[VM] * len(args), out_specs...  20.3 us
  transfers between devices with their start and end apart: 5, of which 3 were waited for; matrix products, arithmetic and copies ran while one was open for 0% of the time, Pallas kernels for 6%

profile of v6, /device:TPU:0, one launch (start us, length us, event | category | flops | bytes accessed | tf_op | source)
XLA Modules:
  0.0 114.8 jit_solution(1540346321230179900)
XLA Ops:
  0.6 0.0 copy-start
  0.6 2.1 %shard_map.103 = (bf16[64,72,128]{2,1,0:T(8,128)(2,1)S(1)}, bf16[64,2048]{1,0:T(8,128)(2,1)S(1)}, bf16[512,2048]{1,0:T(8,128)(2,1)S(1)}) custom-call(bf16[2048,128]{1,0:T(8,128)(2,1)} %feat_hbm.1, s32[1,64]{1,0:T(1,128)} %bitcast.25, s32[1,512]{1,0:T(1,128)} %bitcast.24), custom_call_target="tpu_custom_call" | custom-call | flops 4831838208 | tf_op jit(solution)/shard_map/pallas_call | solution.py:87
  2.8 0.0 copy-start.1
  2.8 31.6 %all_to_all.20.got_ref = bf16[64,72,128]{2,1,0:T(8,128)(2,1)S(1)} all-to-all(bf16[64,72,128]{2,1,0:T(8,128)(2,1)S(1)} %get-tuple-element.18), channel_id=1, replica_groups=mesh['rows'=64,'rep'=2] {'rows'}, dimensions={0} | all-to-all | bytes 2359296 | tf_op jit(solution)/shard_map/all_to_all | solution.py:239
  34.4 0.0 copy-done
  34.4 3.8 %shard_map.105.part_ref = f32[1536,128]{1,0:T(8,128)S(1)} custom-call(bf16[64,72,128]{2,1,0:T(8,128)(2,1)S(1)} %all_to_all.20.got_ref, bf16[2048,4096]{1,0:T(8,128)(2,1)S(1)} %bitcast.8, bf16[2048,512]{1,0:T(8,128)(2,1)S(1)} %bitcast.14), custom_call_target="tpu_custom_call" | custom-call | flops 3623878656 | tf_op jit(solution)/shard_map/pallas_call | solution.py:30
  38.3 0.1 collective-permute-start.1
  38.4 1.4 %shard_map.104.part_ref = f32[512,128]{1,0:T(8,128)S(1)} custom-call(bf16[64,72,128]{2,1,0:T(8,128)(2,1)S(1)} %all_to_all.20.got_ref, bf16[2048,4096]{1,0:T(8,128)(2,1)S(1)} %bitcast.9, bf16[2048,512]{1,0:T(8,128)(2,1)S(1)} %bitcast.15), custom_call_target="tpu_custom_call" | custom-call | flops 1207959552 | tf_op jit(solution)/shard_map/pallas_call | solution.py:30
  39.8 0.6 collective-permute-start
  40.3 0.3 collective-permute-done.1.away_ref
  40.7 0.7 shard_map.106
  41.3 0.2 collective-permute-done.away_ref
  41.5 0.3 shard_map.107
  41.9 0.0 copy-start.3
  41.9 25.6 %all_to_all.21.got_ref = bf16[64,72,128]{2,1,0:T(8,128)(2,1)S(1)} all-to-all(bf16[64,72,128]{2,1,0:T(8,128)(2,1)S(1)} %shard_map.107), channel_id=1, replica_groups=mesh['rows'=64,'rep'=2] {'rows'}, dimensions={0} | all-to-all | bytes 2359296 | tf_op jit(solution)/shard_map/all_to_all | solution.py:239
  67.5 3.3 %shard_map.108 = (f32[1024,256]{1,0:T(8,128)S(1)}, bf16[4096,256]{1,0:T(8,128)(2,1)S(1)}, bf16[512,256]{1,0:T(8,128)(2,1)S(1)}) custom-call(bf16[64,72,128]{2,1,0:T(8,128)(2,1)S(1)} %all_to_all.21.got_ref, bf16[128,256]{1,0:T(8,128)(2,1)S(1)} %copy-done.3, bf16[2048,4096]{1,0:T(8,128)(2,1)S(1)} %bitcast.10, bf16[2048,512]{1,0:T(8,128)(2,1)S(1)} %bitcast.16), custom_call_target="tpu_custom_call" | custom-call | flops 2415919104 | tf_op jit(solution)/shard_map/pallas_call | solution.py:30
  70.7 0.3 collective-permute-start.2
  71.0 0.0 copy-start.2
  71.0 0.0 copy-start.4
  71.0 2.6 %shard_map.109.part_ref = f32[1024,256]{1,0:T(8,128)S(1)} custom-call(bf16[4096,256]{1,0:T(8,128)(2,1)S(1)} %get-tuple-element.23.hid_hub, bf16[512,256]{1,0:T(8,128)(2,1)S(1)} %get-tuple-element.24.hid_slot, bf16[2048,4096]{1,0:T(8,128)(2,1)S(1)} %bitcast.11, bf16[2048,512]{1,0:T(8,128)(2,1)S(1)} %bitcast.17), custom_call_target="tpu_custom_call" | custom-call | flops 2415919104 | tf_op jit(solution)/shard_map/pallas_call | solution.py:30
  73.6 0.0 collective-permute-done.2.away_ref
  73.7 1.2 %shard_map.110 = (bf16[172,1024]{1,0:T(8,128)(2,1)}, bf16[256,1024]{1,0:T(8,128)(2,1)S(1)}, f32[172,256]{1,0:T(8,128)S(1)}) custom-call(f32[1024,256]{1,0:T(8,128)S(1)} %shard_map.109.part_ref, f32[1024,256]{1,0:T(8,128)S(1)} %collective-permute-done.2.away_ref, bf16[172,256]{1,0:T(8,128)(2,1)S(1)} %bitcast.20, s32[1,1024]{1,0:T(1,128)S(1)} %bitcast.21), custom_call_target="tpu_custom_call" | custom-call | tf_op jit(solution)/shard_map/pallas_call | solution.py:30
  74.8 0.5 collective-permute-start.3
  75.3 2.6 %shard_map.111 = (f32[256,4096]{1,0:T(8,128)S(1)}, f32[256,512]{1,0:T(8,128)S(1)}) custom-call(bf16[256,1024]{1,0:T(8,128)(2,1)S(1)} %get-tuple-element.27.dsec_ref, bf16[2048,4096]{1,0:T(8,128)(2,1)S(1)} %bitcast.12, bf16[2048,512]{1,0:T(8,128)(2,1)S(1)} %bitcast.18), custom_call_target="tpu_custom_call" | custom-call | flops 2415919104 | tf_op jit(solution)/shard_map/pallas_call | solution.py:30
  77.9 0.0 collective-permute-done.3.dsec_ref
  77.9 3.6 %shard_map.112 = bf16[64,8,256]{2,1,0:T(8,128)(2,1)S(1)} custom-call(f32[256,4096]{1,0:T(8,128)S(1)} %get-tuple-element.28.hub_own, f32[256,512]{1,0:T(8,128)S(1)} %get-tuple-element.29.slot_own, f32[172,256]{1,0:T(8,128)S(1)} %get-tuple-element.30.grad_ref, bf16[256,1024]{1,0:T(8,128)(2,1)S(1)} %collective-permute-done.3.dsec_ref, ...), custom_call_target="tpu_custom_call" | custom-call | flops 2415919104 | tf_op jit(solution)/shard_map/pallas_call | solution.py:30
  81.5 15.6 %all_to_all.22.got_ref = bf16[64,8,256]{2,1,0:T(8,128)(2,1)S(1)} all-to-all(bf16[64,8,256]{2,1,0:T(8,128)(2,1)S(1)} %shard_map.112), channel_id=1, replica_groups=mesh['rows'=64,'rep'=2] {'rows'}, dimensions={0} | all-to-all | bytes 524288 | tf_op jit(solution)/shard_map/all_to_all | solution.py:239
  97.1 0.1 shard_map.113.mine_ref
  97.2 0.1 collective-permute-start.4
  97.3 1.2 %collective-permute-done.4.away_ref = f32[8,256]{1,0:T(8,128)S(1)} collective-permute-done((f32[8,256]{1,0:T(8,128)S(1)}, f32[8,256]{1,0:T(8,128)S(1)}, u32[]{:S(2)}, u32[]{:S(2)}) %collective-permute-start.4) | collective-permute-done | bytes 8224 | tf_op jit(solution)/shard_map/ppermute | solution.py:242
  98.5 15.6 %all_to_all.23.got_ref = bf16[64,8,256]{2,1,0:T(8,128)(2,1)S(1)} all-to-all(bf16[64,8,256]{2,1,0:T(8,128)(2,1)S(1)} %shard_map.114), channel_id=1, replica_groups=mesh['rows'=64,'rep'=2] {'rows'}, dimensions={0} | all-to-all | bytes 524288 | tf_op jit(solution)/shard_map/all_to_all | solution.py:239
  114.1 0.7 shard_map.115
  (5 shorter events, 0.0 us)
Async XLA Ops:
  0.6 33.8 %copy-start = (bf16[2048,1,4096]{2,0,1:T(8,128)(2,1)S(1)}, bf16[2048,1,4096]{2,0,1:T(8,128)(2,1)}, u32[]{:S(2)}) copy-start(bf16[2048,1,4096]{2,0,1:T(8,128)(2,1)} %param.14) | copy-start | bytes 50331652
  2.8 31.7 %copy-start.1 = (bf16[2048,1,512]{2,0,1:T(8,128)(2,1)S(1)}, bf16[2048,1,512]{2,0,1:T(8,128)(2,1)}, u32[]{:S(2)}) copy-start(bf16[2048,1,512]{2,0,1:T(8,128)(2,1)} %param.15) | copy-start | bytes 6291460
  38.3 2.4 %collective-permute-start.1 = (f32[1536,128]{1,0:T(8,128)S(1)}, f32[1536,128]{1,0:T(8,128)S(1)}, u32[]{:S(2)}, u32[]{:S(2)}) collective-permute-start(f32[1536,128]{1,0:T(8,128)S(1)} %shard_map.105.part_ref), channel_id=1, source_target_pairs={{0,1},{1,0},{2,3},{3,2},{4,5},{5,4},{6,7},{7,6},{8,9},{9,8},{10,11... | collective-permute-start | bytes 2359304 | tf_op jit(solution)/shard_map/ppermute | solution.py:242
  39.8 1.7 %collective-permute-start = (f32[512,128]{1,0:T(8,128)S(1)}, f32[512,128]{1,0:T(8,128)S(1)}, u32[]{:S(2)}, u32[]{:S(2)}) collective-permute-start(f32[512,128]{1,0:T(8,128)S(1)} %shard_map.104.part_ref), channel_id=1, source_target_pairs={{0,1},{1,0},{2,3},{3,2},{4,5},{5,4},{6,7},{7,6},{8,9},{9,8},{10,11... | collective-permute-start | bytes 786440 | tf_op jit(solution)/shard_map/ppermute | solution.py:242
  41.9 25.6 %copy-start.3 = (bf16[128,256]{1,0:T(8,128)(2,1)S(1)}, bf16[128,256]{1,0:T(8,128)(2,1)}, u32[]{:S(2)}) copy-start(bf16[128,256]{1,0:T(8,128)(2,1)} %w_ref.1) | copy-start | bytes 196612
  70.7 2.9 %collective-permute-start.2 = (f32[1024,256]{1,0:T(8,128)S(1)}, f32[1024,256]{1,0:T(8,128)S(1)}, u32[]{:S(2)}, u32[]{:S(2)}) collective-permute-start(f32[1024,256]{1,0:T(8,128)S(1)} %get-tuple-element.25), channel_id=1, source_target_pairs={{0,1},{1,0},{2,3},{3,2},{4,5},{5,4},{6,7},{7,6},{8,9},{9,8},{10,11... | collective-permute-start | bytes 3145736 | tf_op jit(solution)/shard_map/ppermute | solution.py:242
  71.0 2.6 %copy-start.2 = (bf16[256,172]{0,1:T(8,128)(2,1)S(1)}, bf16[256,172]{0,1:T(8,128)(2,1)}, u32[]{:S(2)}) copy-start(bf16[256,172]{0,1:T(8,128)(2,1)} %param.10) | copy-start | bytes 264196
  71.0 2.6 %copy-start.4 = (s32[1024]{0:T(1024)S(1)}, s32[1024]{0:T(1024)}, u32[]{:S(2)}) copy-start(s32[1024]{0:T(1024)} %param.11) | copy-start | bytes 12292
  74.8 3.1 %collective-permute-start.3 = (bf16[256,1024]{1,0:T(8,128)(2,1)S(1)}, bf16[256,1024]{1,0:T(8,128)(2,1)S(1)}, u32[]{:S(2)}, u32[]{:S(2)}) collective-permute-start(bf16[256,1024]{1,0:T(8,128)(2,1)S(1)} %get-tuple-element.27.dsec_ref), channel_id=1, source_target_pairs={{0,1},{1,0},{2,3},{3,2},{4,5},{5,4},{6,7},{7,6},{8,9},{9,8},{10,11... | collective-permute-start | bytes 1572872 | tf_op jit(solution)/shard_map/ppermute | solution.py:242
  97.2 1.2 %collective-permute-start.4 = (f32[8,256]{1,0:T(8,128)S(1)}, f32[8,256]{1,0:T(8,128)S(1)}, u32[]{:S(2)}, u32[]{:S(2)}) collective-permute-start(f32[8,256]{1,0:T(8,128)S(1)} %shard_map.113.mine_ref), channel_id=1, source_target_pairs={{0,1},{1,0},{2,3},{3,2},{4,5},{5,4},{6,7},{7,6},{8,9},{9,8},{10,11... | collective-permute-start | bytes 24584 | tf_op jit(solution)/shard_map/ppermute | solution.py:242

commit v7 on v6

--- a/solution.py
+++ b/solution.py
@@ -4,9 +4,12 @@
 from jax import lax
 from jax.experimental import pallas as pl
 from jax.experimental.pallas import tpu as pltpu
+from jax.sharding import Mesh
 from jax.sharding import PartitionSpec as P
 
 SWAP = [(0, 1), (1, 0)]
+ROWS = ("z", "x", "y")
+NEAR, FAR = ("y", "rep"), ("z", "x")
 F32, BF16 = jnp.float32, jnp.bfloat16
 VM = pl.BlockSpec(memory_space=pltpu.VMEM)
 MIB = 1024 * 1024
@@ -202,13 +205,9 @@
     out_ref[...] = flat.reshape(out_ref.shape).astype(BF16)
 
 
-def sum_body(got_ref, out_ref):
-    out_ref[...] = jnp.sum(got_ref[...].astype(F32), axis=0)
-
-
-def share_body(mine_ref, away_ref, out_ref):
-    mine = (mine_ref[...] + away_ref[...]).astype(BF16).astype(F32)
-    out_ref[...] = jnp.broadcast_to(mine[None], out_ref.shape).astype(BF16)
+def fold_body(got_ref, out_ref):
+    total = jnp.sum(got_ref[...].astype(F32), axis=0).astype(BF16).astype(F32)
+    out_ref[...] = jnp.broadcast_to(total[None], out_ref.shape).astype(BF16)
 
 
 def parts_body(got_ref, in_ref, out_ref):
@@ -220,7 +219,7 @@
 
 
 def on_device(node_feats, w_in, w_out, labels, hub_rows, send_rows, adj_hub, adj_sparse):
-    nrows = lax.axis_size("rows")
+    nrows = lax.axis_size(ROWS)
     slab, width = node_feats.shape
     half = slab // lax.axis_size("rep")
     hid, classes = w_out.shape
@@ -235,8 +234,8 @@
     packet = shape((nrows, hubs + slots, width), BF16)
     products = 2 * slab * (hub_cols + slot_cols)
 
-    def exchange(x):
-        return lax.all_to_all(x, "rows", split_axis=0, concat_axis=0, tiled=True)
+    def exchange(x, axes=ROWS):
+        return lax.all_to_all(x, axes, split_axis=0, concat_axis=0, tiled=True)
 
     def swap(x):
         return lax.ppermute(x, "rep", SWAP)
@@ -284,32 +283,36 @@
         flops=products * hid // 2,
     )
     count = width + classes
-    share = -(-count // (8 * nrows)) * 8
+    near, far = lax.axis_size(NEAR), lax.axis_size(FAR)
+    share = -(-count // (8 * near)) * 8
     flat = call(
-        functools.partial(back_away_body, hubs, STEP4), shape((nrows, share, hid), BF16),
+        functools.partial(back_away_body, hubs, STEP4), shape((near, share, hid), BF16),
         hub_own, slot_own, grad_out, oth, got, hid_hub, hid_slot, hub_mat, sparse_mat,
         scratch=[pltpu.VMEM((hid, width), F32)], flops=products * hid // 2,
     )
-    mine = call(sum_body, shape((share, hid), F32), exchange(flat))
-    whole = exchange(call(share_body, shape((nrows, share, hid), BF16), mine, swap(mine)))
+    piece = call(fold_body, shape((far, share, hid), BF16), exchange(flat, NEAR))
+    whole = exchange(call(fold_body, shape((near, share, hid), BF16), exchange(piece, FAR)), NEAR)
     grad_in, grad_out = call(parts_body, (shape((width, hid), F32), shape((classes, hid), F32)), whole)
     return (logits.T, grad_in, grad_out.T)
 
 
 def solution(mesh):
+    rows, cores = mesh.devices.shape
+    side = round(rows ** (1 / 3))
+    cube = Mesh(mesh.devices.reshape(-1, side, side, cores), ("z", "x", "y", "rep"))
     return jax.shard_map(
         on_device,
-        mesh=mesh,
+        mesh=cube,
         in_specs=(
-            P("rows", None),
+            P(ROWS, None),
             P(),
             P(),
-            P(("rows", "rep")),
-            P("rows", "rep", None),
-            P("rows", "rep", None),
-            P("rows", "rep", None),
-            P("rows", "rep", None),
+            P((*ROWS, "rep")),
+            P(ROWS, "rep", None),
+            P(ROWS, "rep", None),
+            P(ROWS, "rep", None),
+            P(ROWS, "rep", None),
         ),
-        out_specs=(P(("rows", "rep"), None), P(), P()),
+        out_specs=(P((*ROWS, "rep"), None), P(), P()),
         check_vma=False,
     )

time: 115 us -> 113 us (0.983)
    ppermute x5 -> x4, waiting for transfers between devices: 1.65 us -> 0.5 us  [swap(): return lax.ppermute(x, 'rep', SWAP)]
    all_to_all x4 -> x5, blocking collectives: 88.4 us -> 87.3 us  [exchange(): return lax.all_to_all(x, axes, split_axis=0, concat_axis=0, tiled=True)]
  transfers between devices with their start and end apart: 5 -> 4, of which waited for: 3 -> 2; matrix products, arithmetic and copies ran while one was open for 0% -> 0% of each run, Pallas kernels for 6% -> 6%
where the time goes in v7:
time: 113 us; the launch traced here: 112 us
  blocking collectives  87.3 us (77%)
  Pallas kernels  22.4 us (20%)
  starting transfers between devices  1.4 us (1%)
    all_to_all x5, blocking collectives, exchange(): return lax.all_to_all(x, axes, split_axis=0, concat_axis=0, tiled=True)  87.3 us
    pallas_call x12, Pallas kernels, call(): pl.pallas_call(body, out_shape=outs, in_specs=[VM] * len(args), out_specs...  20.3 us
  transfers between devices with their start and end apart: 4, of which 2 were waited for; matrix products, arithmetic and copies ran while one was open for 0% of the time, Pallas kernels for 6%

profile of v7, /device:TPU:0, one launch (start us, length us, event | category | flops | bytes accessed | tf_op | source)
XLA Modules:
  0.0 112.4 jit_solution(248670045545946320)
XLA Ops:
  0.6 0.0 copy-start
  0.6 2.1 %shard_map.103 = (bf16[64,72,128]{2,1,0:T(8,128)(2,1)S(1)}, bf16[64,2048]{1,0:T(8,128)(2,1)S(1)}, bf16[512,2048]{1,0:T(8,128)(2,1)S(1)}) custom-call(bf16[2048,128]{1,0:T(8,128)(2,1)} %feat_hbm.1, s32[1,64]{1,0:T(1,128)} %bitcast.25, s32[1,512]{1,0:T(1,128)} %bitcast.24), custom_call_target="tpu_custom_call" | custom-call | flops 4831838208 | tf_op jit(solution)/shard_map/pallas_call | solution.py:90
  2.8 0.0 copy-start.1
  2.8 31.6 %all_to_all.25.got_ref = bf16[64,72,128]{2,1,0:T(8,128)(2,1)S(1)} all-to-all(bf16[64,72,128]{2,1,0:T(8,128)(2,1)S(1)} %get-tuple-element.18), channel_id=1, replica_groups=mesh['z'=4,'x'=4,'y'=4,'rep'=2] {'z','x','y'}, dimensions={0} | all-to-all | bytes 2359296 | tf_op jit(solution)/shard_map/all_to_all | solution.py:238
  34.4 0.0 copy-done
  34.4 0.0 copy-done.1
  34.4 3.8 %shard_map.105.part_ref = f32[1536,128]{1,0:T(8,128)S(1)} custom-call(bf16[64,72,128]{2,1,0:T(8,128)(2,1)S(1)} %all_to_all.25.got_ref, bf16[2048,4096]{1,0:T(8,128)(2,1)S(1)} %bitcast.8, bf16[2048,512]{1,0:T(8,128)(2,1)S(1)} %bitcast.14), custom_call_target="tpu_custom_call" | custom-call | flops 3623878656 | tf_op jit(solution)/shard_map/pallas_call | solution.py:33
  38.3 0.1 collective-permute-start.1
  38.4 1.4 %shard_map.104.part_ref = f32[512,128]{1,0:T(8,128)S(1)} custom-call(bf16[64,72,128]{2,1,0:T(8,128)(2,1)S(1)} %all_to_all.25.got_ref, bf16[2048,4096]{1,0:T(8,128)(2,1)S(1)} %bitcast.9, bf16[2048,512]{1,0:T(8,128)(2,1)S(1)} %bitcast.15), custom_call_target="tpu_custom_call" | custom-call | flops 1207959552 | tf_op jit(solution)/shard_map/pallas_call | solution.py:33
  39.8 0.6 collective-permute-start
  40.3 0.3 collective-permute-done.1.away_ref
  40.7 0.7 shard_map.106
  41.3 0.2 collective-permute-done.away_ref
  41.5 0.3 shard_map.107
  41.9 0.0 copy-start.3
  41.9 25.6 %all_to_all.26.got_ref = bf16[64,72,128]{2,1,0:T(8,128)(2,1)S(1)} all-to-all(bf16[64,72,128]{2,1,0:T(8,128)(2,1)S(1)} %shard_map.107), channel_id=1, replica_groups=mesh['z'=4,'x'=4,'y'=4,'rep'=2] {'z','x','y'}, dimensions={0} | all-to-all | bytes 2359296 | tf_op jit(solution)/shard_map/all_to_all | solution.py:238
  67.5 3.3 %shard_map.108 = (f32[1024,256]{1,0:T(8,128)S(1)}, bf16[4096,256]{1,0:T(8,128)(2,1)S(1)}, bf16[512,256]{1,0:T(8,128)(2,1)S(1)}) custom-call(bf16[64,72,128]{2,1,0:T(8,128)(2,1)S(1)} %all_to_all.26.got_ref, bf16[128,256]{1,0:T(8,128)(2,1)S(1)} %copy-done.3, bf16[2048,4096]{1,0:T(8,128)(2,1)S(1)} %bitcast.10, bf16[2048,512]{1,0:T(8,128)(2,1)S(1)} %bitcast.16), custom_call_target="tpu_custom_call" | custom-call | flops 2415919104 | tf_op jit(solution)/shard_map/pallas_call | solution.py:33
  70.7 0.3 collective-permute-start.2
  71.0 0.0 copy-start.2
  71.0 0.0 copy-start.4
  71.0 2.6 %shard_map.109.part_ref = f32[1024,256]{1,0:T(8,128)S(1)} custom-call(bf16[4096,256]{1,0:T(8,128)(2,1)S(1)} %get-tuple-element.23.hid_hub, bf16[512,256]{1,0:T(8,128)(2,1)S(1)} %get-tuple-element.24.hid_slot, bf16[2048,4096]{1,0:T(8,128)(2,1)S(1)} %bitcast.11, bf16[2048,512]{1,0:T(8,128)(2,1)S(1)} %bitcast.17), custom_call_target="tpu_custom_call" | custom-call | flops 2415919104 | tf_op jit(solution)/shard_map/pallas_call | solution.py:33
  73.6 0.0 collective-permute-done.2.away_ref
  73.7 1.2 %shard_map.110 = (bf16[172,1024]{1,0:T(8,128)(2,1)}, bf16[256,1024]{1,0:T(8,128)(2,1)S(1)}, f32[172,256]{1,0:T(8,128)S(1)}) custom-call(f32[1024,256]{1,0:T(8,128)S(1)} %shard_map.109.part_ref, f32[1024,256]{1,0:T(8,128)S(1)} %collective-permute-done.2.away_ref, bf16[172,256]{1,0:T(8,128)(2,1)S(1)} %bitcast.20, s32[1,1024]{1,0:T(1,128)S(1)} %bitcast.21), custom_call_target="tpu_custom_call" | custom-call | tf_op jit(solution)/shard_map/pallas_call | solution.py:33
  74.8 0.5 collective-permute-start.3
  75.3 2.6 %shard_map.111 = (f32[256,4096]{1,0:T(8,128)S(1)}, f32[256,512]{1,0:T(8,128)S(1)}) custom-call(bf16[256,1024]{1,0:T(8,128)(2,1)S(1)} %get-tuple-element.27.dsec_ref, bf16[2048,4096]{1,0:T(8,128)(2,1)S(1)} %bitcast.12, bf16[2048,512]{1,0:T(8,128)(2,1)S(1)} %bitcast.18), custom_call_target="tpu_custom_call" | custom-call | flops 2415919104 | tf_op jit(solution)/shard_map/pallas_call | solution.py:33
  77.9 0.0 collective-permute-done.3.dsec_ref
  77.9 3.6 %shard_map.112 = bf16[8,40,256]{2,1,0:T(8,128)(2,1)S(1)} custom-call(f32[256,4096]{1,0:T(8,128)S(1)} %get-tuple-element.28.hub_own, f32[256,512]{1,0:T(8,128)S(1)} %get-tuple-element.29.slot_own, f32[172,256]{1,0:T(8,128)S(1)} %get-tuple-element.30.grad_ref, bf16[256,1024]{1,0:T(8,128)(2,1)S(1)} %collective-permute-done.3.dsec_ref, ...), custom_call_target="tpu_custom_call" | custom-call | flops 2415919104 | tf_op jit(solution)/shard_map/pallas_call | solution.py:33
  81.5 8.9 %all_to_all.27.got_ref = bf16[8,40,256]{2,1,0:T(8,128)(2,1)S(1)} all-to-all(bf16[8,40,256]{2,1,0:T(8,128)(2,1)S(1)} %shard_map.112), channel_id=1, replica_groups=mesh['z'=4,'x'=4,'y'=4,'rep'=2] {'y','rep'}, dimensions={0} | all-to-all | bytes 327680 | tf_op jit(solution)/shard_map/all_to_all | solution.py:238
  90.4 12.4 %all_to_all.28.got_ref = bf16[16,40,256]{2,1,0:T(8,128)(2,1)S(1)} all-to-all(bf16[16,40,256]{2,1,0:T(8,128)(2,1)S(1)} %shard_map.113), channel_id=1, replica_groups=mesh['z'=4,'x'=4,'y'=4,'rep'=2] {'z','x'}, dimensions={0} | all-to-all | bytes 655360 | tf_op jit(solution)/shard_map/all_to_all | solution.py:238
  102.8 0.1 shard_map.114
  102.8 8.9 %all_to_all.29.got_ref = bf16[8,40,256]{2,1,0:T(8,128)(2,1)S(1)} all-to-all(bf16[8,40,256]{2,1,0:T(8,128)(2,1)S(1)} %shard_map.114), channel_id=1, replica_groups=mesh['z'=4,'x'=4,'y'=4,'rep'=2] {'y','rep'}, dimensions={0} | all-to-all | bytes 327680 | tf_op jit(solution)/shard_map/all_to_all | solution.py:238
  111.7 0.7 shard_map.115
  (4 shorter events, 0.0 us)
Async XLA Ops:
  0.6 33.8 %copy-start = (bf16[2048,1,4096]{2,0,1:T(8,128)(2,1)S(1)}, bf16[2048,1,4096]{2,0,1:T(8,128)(2,1)}, u32[]{:S(2)}) copy-start(bf16[2048,1,4096]{2,0,1:T(8,128)(2,1)} %param.14) | copy-start | bytes 50331652
  2.8 31.7 %copy-start.1 = (bf16[2048,1,512]{2,0,1:T(8,128)(2,1)S(1)}, bf16[2048,1,512]{2,0,1:T(8,128)(2,1)}, u32[]{:S(2)}) copy-start(bf16[2048,1,512]{2,0,1:T(8,128)(2,1)} %param.15) | copy-start | bytes 6291460
  38.3 2.4 %collective-permute-start.1 = (f32[1536,128]{1,0:T(8,128)S(1)}, f32[1536,128]{1,0:T(8,128)S(1)}, u32[]{:S(2)}, u32[]{:S(2)}) collective-permute-start(f32[1536,128]{1,0:T(8,128)S(1)} %shard_map.105.part_ref), channel_id=1, source_target_pairs={{0,1},{1,0},{2,3},{3,2},{4,5},{5,4},{6,7},{7,6},{8,9},{9,8},{10,11... | collective-permute-start | bytes 2359304 | tf_op jit(solution)/shard_map/ppermute | solution.py:241
  39.8 1.7 %collective-permute-start = (f32[512,128]{1,0:T(8,128)S(1)}, f32[512,128]{1,0:T(8,128)S(1)}, u32[]{:S(2)}, u32[]{:S(2)}) collective-permute-start(f32[512,128]{1,0:T(8,128)S(1)} %shard_map.104.part_ref), channel_id=1, source_target_pairs={{0,1},{1,0},{2,3},{3,2},{4,5},{5,4},{6,7},{7,6},{8,9},{9,8},{10,11... | collective-permute-start | bytes 786440 | tf_op jit(solution)/shard_map/ppermute | solution.py:241
  41.9 25.6 %copy-start.3 = (bf16[128,256]{1,0:T(8,128)(2,1)S(1)}, bf16[128,256]{1,0:T(8,128)(2,1)}, u32[]{:S(2)}) copy-start(bf16[128,256]{1,0:T(8,128)(2,1)} %w_ref.1) | copy-start | bytes 196612
  70.7 2.9 %collective-permute-start.2 = (f32[1024,256]{1,0:T(8,128)S(1)}, f32[1024,256]{1,0:T(8,128)S(1)}, u32[]{:S(2)}, u32[]{:S(2)}) collective-permute-start(f32[1024,256]{1,0:T(8,128)S(1)} %get-tuple-element.25), channel_id=1, source_target_pairs={{0,1},{1,0},{2,3},{3,2},{4,5},{5,4},{6,7},{7,6},{8,9},{9,8},{10,11... | collective-permute-start | bytes 3145736 | tf_op jit(solution)/shard_map/ppermute | solution.py:241
  71.0 2.6 %copy-start.2 = (bf16[256,172]{0,1:T(8,128)(2,1)S(1)}, bf16[256,172]{0,1:T(8,128)(2,1)}, u32[]{:S(2)}) copy-start(bf16[256,172]{0,1:T(8,128)(2,1)} %param.10) | copy-start | bytes 264196
  71.0 2.6 %copy-start.4 = (s32[1024]{0:T(1024)S(1)}, s32[1024]{0:T(1024)}, u32[]{:S(2)}) copy-start(s32[1024]{0:T(1024)} %param.11) | copy-start | bytes 12292
  74.8 3.1 %collective-permute-start.3 = (bf16[256,1024]{1,0:T(8,128)(2,1)S(1)}, bf16[256,1024]{1,0:T(8,128)(2,1)S(1)}, u32[]{:S(2)}, u32[]{:S(2)}) collective-permute-start(bf16[256,1024]{1,0:T(8,128)(2,1)S(1)} %get-tuple-element.27.dsec_ref), channel_id=1, source_target_pairs={{0,1},{1,0},{2,3},{3,2},{4,5},{5,4},{6,7},{7,6},{8,9},{9,8},{10,11... | collective-permute-start | bytes 1572872 | tf_op jit(solution)/shard_map/ppermute | solution.py:241

commit v8 on v7

--- a/solution.py
+++ b/solution.py
@@ -15,8 +15,8 @@
 MIB = 1024 * 1024
 PIECES = 1
 TOP = 6
-STEP1 = 1024
-STEP2 = 512
+STEP1 = 256
+STEP2 = 256
 STEP3 = 4096
 STEP4 = 2048
 

time: 113 us -> 113 us (level)
  no operation moved by 1% of the time
where the time goes in v8:
time: 113 us; the launch traced here: 112 us
  blocking collectives  87.3 us (77%)
  Pallas kernels  22.4 us (20%)
  starting transfers between devices  1.4 us (1%)
    all_to_all x5, blocking collectives, exchange(): return lax.all_to_all(x, axes, split_axis=0, concat_axis=0, tiled=True)  87.3 us
    pallas_call x12, Pallas kernels, call(): pl.pallas_call(body, out_shape=outs, in_specs=[VM] * len(args), out_specs...  20.2 us
  transfers between devices with their start and end apart: 4, of which 2 were waited for; matrix products, arithmetic and copies ran while one was open for 0% of the time, Pallas kernels for 6%

profile of v8, /device:TPU:0, one launch (start us, length us, event | category | flops | bytes accessed | tf_op | source)
XLA Modules:
  0.0 112.4 jit_solution(182800739917897170)
XLA Ops:
  0.6 0.0 copy-start
  0.6 2.1 %shard_map.103 = (bf16[64,72,128]{2,1,0:T(8,128)(2,1)S(1)}, bf16[64,2048]{1,0:T(8,128)(2,1)S(1)}, bf16[512,2048]{1,0:T(8,128)(2,1)S(1)}) custom-call(bf16[2048,128]{1,0:T(8,128)(2,1)} %feat_hbm.1, s32[1,64]{1,0:T(1,128)} %bitcast.25, s32[1,512]{1,0:T(1,128)} %bitcast.24), custom_call_target="tpu_custom_call" | custom-call | flops 4831838208 | tf_op jit(solution)/shard_map/pallas_call | solution.py:90
  2.8 0.0 copy-start.1
  2.8 31.6 %all_to_all.25.got_ref = bf16[64,72,128]{2,1,0:T(8,128)(2,1)S(1)} all-to-all(bf16[64,72,128]{2,1,0:T(8,128)(2,1)S(1)} %get-tuple-element.18), channel_id=1, replica_groups=mesh['z'=4,'x'=4,'y'=4,'rep'=2] {'z','x','y'}, dimensions={0} | all-to-all | bytes 2359296 | tf_op jit(solution)/shard_map/all_to_all | solution.py:238
  34.4 0.0 copy-done
  34.4 0.0 copy-done.1
  34.4 3.8 %shard_map.105.part_ref = f32[1536,128]{1,0:T(8,128)S(1)} custom-call(bf16[64,72,128]{2,1,0:T(8,128)(2,1)S(1)} %all_to_all.25.got_ref, bf16[2048,4096]{1,0:T(8,128)(2,1)S(1)} %bitcast.8, bf16[2048,512]{1,0:T(8,128)(2,1)S(1)} %bitcast.14), custom_call_target="tpu_custom_call" | custom-call | flops 3623878656 | tf_op jit(solution)/shard_map/pallas_call | solution.py:33
  38.3 0.1 collective-permute-start.1
  38.4 1.4 %shard_map.104.part_ref = f32[512,128]{1,0:T(8,128)S(1)} custom-call(bf16[64,72,128]{2,1,0:T(8,128)(2,1)S(1)} %all_to_all.25.got_ref, bf16[2048,4096]{1,0:T(8,128)(2,1)S(1)} %bitcast.9, bf16[2048,512]{1,0:T(8,128)(2,1)S(1)} %bitcast.15), custom_call_target="tpu_custom_call" | custom-call | flops 1207959552 | tf_op jit(solution)/shard_map/pallas_call | solution.py:33
  39.8 0.6 collective-permute-start
  40.3 0.3 collective-permute-done.1.away_ref
  40.7 0.7 shard_map.106
  41.3 0.2 collective-permute-done.away_ref
  41.5 0.3 shard_map.107
  41.9 0.0 copy-start.3
  41.9 25.6 %all_to_all.26.got_ref = bf16[64,72,128]{2,1,0:T(8,128)(2,1)S(1)} all-to-all(bf16[64,72,128]{2,1,0:T(8,128)(2,1)S(1)} %shard_map.107), channel_id=1, replica_groups=mesh['z'=4,'x'=4,'y'=4,'rep'=2] {'z','x','y'}, dimensions={0} | all-to-all | bytes 2359296 | tf_op jit(solution)/shard_map/all_to_all | solution.py:238
  67.5 3.3 %shard_map.108 = (f32[1024,256]{1,0:T(8,128)S(1)}, bf16[4096,256]{1,0:T(8,128)(2,1)S(1)}, bf16[512,256]{1,0:T(8,128)(2,1)S(1)}) custom-call(bf16[64,72,128]{2,1,0:T(8,128)(2,1)S(1)} %all_to_all.26.got_ref, bf16[128,256]{1,0:T(8,128)(2,1)S(1)} %copy-done.3, bf16[2048,4096]{1,0:T(8,128)(2,1)S(1)} %bitcast.10, bf16[2048,512]{1,0:T(8,128)(2,1)S(1)} %bitcast.16), custom_call_target="tpu_custom_call" | custom-call | flops 2415919104 | tf_op jit(solution)/shard_map/pallas_call | solution.py:33
  70.7 0.3 collective-permute-start.2
  71.0 0.0 copy-start.2
  71.0 0.0 copy-start.4
  71.0 2.6 %shard_map.109.part_ref = f32[1024,256]{1,0:T(8,128)S(1)} custom-call(bf16[4096,256]{1,0:T(8,128)(2,1)S(1)} %get-tuple-element.23.hid_hub, bf16[512,256]{1,0:T(8,128)(2,1)S(1)} %get-tuple-element.24.hid_slot, bf16[2048,4096]{1,0:T(8,128)(2,1)S(1)} %bitcast.11, bf16[2048,512]{1,0:T(8,128)(2,1)S(1)} %bitcast.17), custom_call_target="tpu_custom_call" | custom-call | flops 2415919104 | tf_op jit(solution)/shard_map/pallas_call | solution.py:33
  73.6 0.0 collective-permute-done.2.away_ref
  73.6 1.2 %shard_map.110 = (bf16[172,1024]{1,0:T(8,128)(2,1)}, bf16[256,1024]{1,0:T(8,128)(2,1)S(1)}, f32[172,256]{1,0:T(8,128)S(1)}) custom-call(f32[1024,256]{1,0:T(8,128)S(1)} %shard_map.109.part_ref, f32[1024,256]{1,0:T(8,128)S(1)} %collective-permute-done.2.away_ref, bf16[172,256]{1,0:T(8,128)(2,1)S(1)} %bitcast.20, s32[1,1024]{1,0:T(1,128)S(1)} %bitcast.21), custom_call_target="tpu_custom_call" | custom-call | tf_op jit(solution)/shard_map/pallas_call | solution.py:33
  74.8 0.5 collective-permute-start.3
  75.3 2.6 %shard_map.111 = (f32[256,4096]{1,0:T(8,128)S(1)}, f32[256,512]{1,0:T(8,128)S(1)}) custom-call(bf16[256,1024]{1,0:T(8,128)(2,1)S(1)} %get-tuple-element.27.dsec_ref, bf16[2048,4096]{1,0:T(8,128)(2,1)S(1)} %bitcast.12, bf16[2048,512]{1,0:T(8,128)(2,1)S(1)} %bitcast.18), custom_call_target="tpu_custom_call" | custom-call | flops 2415919104 | tf_op jit(solution)/shard_map/pallas_call | solution.py:33
  77.9 0.0 collective-permute-done.3.dsec_ref
  77.9 3.6 %shard_map.112 = bf16[8,40,256]{2,1,0:T(8,128)(2,1)S(1)} custom-call(f32[256,4096]{1,0:T(8,128)S(1)} %get-tuple-element.28.hub_own, f32[256,512]{1,0:T(8,128)S(1)} %get-tuple-element.29.slot_own, f32[172,256]{1,0:T(8,128)S(1)} %get-tuple-element.30.grad_ref, bf16[256,1024]{1,0:T(8,128)(2,1)S(1)} %collective-permute-done.3.dsec_ref, ...), custom_call_target="tpu_custom_call" | custom-call | flops 2415919104 | tf_op jit(solution)/shard_map/pallas_call | solution.py:33
  81.5 8.9 %all_to_all.27.got_ref = bf16[8,40,256]{2,1,0:T(8,128)(2,1)S(1)} all-to-all(bf16[8,40,256]{2,1,0:T(8,128)(2,1)S(1)} %shard_map.112), channel_id=1, replica_groups=mesh['z'=4,'x'=4,'y'=4,'rep'=2] {'y','rep'}, dimensions={0} | all-to-all | bytes 327680 | tf_op jit(solution)/shard_map/all_to_all | solution.py:238
  90.4 12.4 %all_to_all.28.got_ref = bf16[16,40,256]{2,1,0:T(8,128)(2,1)S(1)} all-to-all(bf16[16,40,256]{2,1,0:T(8,128)(2,1)S(1)} %shard_map.113), channel_id=1, replica_groups=mesh['z'=4,'x'=4,'y'=4,'rep'=2] {'z','x'}, dimensions={0} | all-to-all | bytes 655360 | tf_op jit(solution)/shard_map/all_to_all | solution.py:238
  102.8 0.1 shard_map.114
  102.8 8.9 %all_to_all.29.got_ref = bf16[8,40,256]{2,1,0:T(8,128)(2,1)S(1)} all-to-all(bf16[8,40,256]{2,1,0:T(8,128)(2,1)S(1)} %shard_map.114), channel_id=1, replica_groups=mesh['z'=4,'x'=4,'y'=4,'rep'=2] {'y','rep'}, dimensions={0} | all-to-all | bytes 327680 | tf_op jit(solution)/shard_map/all_to_all | solution.py:238
  111.7 0.7 shard_map.115
  (4 shorter events, 0.0 us)
Async XLA Ops:
  0.6 33.8 %copy-start = (bf16[2048,1,4096]{2,0,1:T(8,128)(2,1)S(1)}, bf16[2048,1,4096]{2,0,1:T(8,128)(2,1)}, u32[]{:S(2)}) copy-start(bf16[2048,1,4096]{2,0,1:T(8,128)(2,1)} %param.14) | copy-start | bytes 50331652
  2.8 31.7 %copy-start.1 = (bf16[2048,1,512]{2,0,1:T(8,128)(2,1)S(1)}, bf16[2048,1,512]{2,0,1:T(8,128)(2,1)}, u32[]{:S(2)}) copy-start(bf16[2048,1,512]{2,0,1:T(8,128)(2,1)} %param.15) | copy-start | bytes 6291460
  38.3 2.4 %collective-permute-start.1 = (f32[1536,128]{1,0:T(8,128)S(1)}, f32[1536,128]{1,0:T(8,128)S(1)}, u32[]{:S(2)}, u32[]{:S(2)}) collective-permute-start(f32[1536,128]{1,0:T(8,128)S(1)} %shard_map.105.part_ref), channel_id=1, source_target_pairs={{0,1},{1,0},{2,3},{3,2},{4,5},{5,4},{6,7},{7,6},{8,9},{9,8},{10,11... | collective-permute-start | bytes 2359304 | tf_op jit(solution)/shard_map/ppermute | solution.py:241
  39.8 1.7 %collective-permute-start = (f32[512,128]{1,0:T(8,128)S(1)}, f32[512,128]{1,0:T(8,128)S(1)}, u32[]{:S(2)}, u32[]{:S(2)}) collective-permute-start(f32[512,128]{1,0:T(8,128)S(1)} %shard_map.104.part_ref), channel_id=1, source_target_pairs={{0,1},{1,0},{2,3},{3,2},{4,5},{5,4},{6,7},{7,6},{8,9},{9,8},{10,11... | collective-permute-start | bytes 786440 | tf_op jit(solution)/shard_map/ppermute | solution.py:241
  41.9 25.6 %copy-start.3 = (bf16[128,256]{1,0:T(8,128)(2,1)S(1)}, bf16[128,256]{1,0:T(8,128)(2,1)}, u32[]{:S(2)}) copy-start(bf16[128,256]{1,0:T(8,128)(2,1)} %w_ref.1) | copy-start | bytes 196612
  70.7 2.9 %collective-permute-start.2 = (f32[1024,256]{1,0:T(8,128)S(1)}, f32[1024,256]{1,0:T(8,128)S(1)}, u32[]{:S(2)}, u32[]{:S(2)}) collective-permute-start(f32[1024,256]{1,0:T(8,128)S(1)} %get-tuple-element.25), channel_id=1, source_target_pairs={{0,1},{1,0},{2,3},{3,2},{4,5},{5,4},{6,7},{7,6},{8,9},{9,8},{10,11... | collective-permute-start | bytes 3145736 | tf_op jit(solution)/shard_map/ppermute | solution.py:241
  71.0 2.6 %copy-start.2 = (bf16[256,172]{0,1:T(8,128)(2,1)S(1)}, bf16[256,172]{0,1:T(8,128)(2,1)}, u32[]{:S(2)}) copy-start(bf16[256,172]{0,1:T(8,128)(2,1)} %param.10) | copy-start | bytes 264196
  71.0 2.6 %copy-start.4 = (s32[1024]{0:T(1024)S(1)}, s32[1024]{0:T(1024)}, u32[]{:S(2)}) copy-start(s32[1024]{0:T(1024)} %param.11) | copy-start | bytes 12292
  74.8 3.1 %collective-permute-start.3 = (bf16[256,1024]{1,0:T(8,128)(2,1)S(1)}, bf16[256,1024]{1,0:T(8,128)(2,1)S(1)}, u32[]{:S(2)}, u32[]{:S(2)}) collective-permute-start(bf16[256,1024]{1,0:T(8,128)(2,1)S(1)} %get-tuple-element.27.dsec_ref), channel_id=1, source_target_pairs={{0,1},{1,0},{2,3},{3,2},{4,5},{5,4},{6,7},{7,6},{8,9},{9,8},{10,11... | collective-permute-start | bytes 1572872 | tf_op jit(solution)/shard_map/ppermute | solution.py:241

commit v9 on v8

--- a/solution.py
+++ b/solution.py
@@ -125,8 +125,9 @@
 
 def first_body(hubs, start, got_ref, hub_mat, sparse_mat, part_ref):
     hub, slot = split(got_ref, hubs)
-    at = pl.ds(start, part_ref.shape[0])
-    part_ref[...] = dot(hub_mat[at, :], hub) + dot(sparse_mat[at, :], slot)
+    for i in range(part_ref.shape[0] // STEP1):
+        at = pl.ds(start + i * STEP1, STEP1)
+        part_ref[pl.ds(i * STEP1, STEP1), :] = dot(hub_mat[at, :], hub) + dot(sparse_mat[at, :], slot)
 
 
 def second_rows(step, start, part_ref, hid_hub, hid_slot, hub_mat, sparse_mat):

time: 113 us -> 113 us (level)
  no operation moved by 1% of the time
where the time goes in v9:
time: 113 us; the launch traced here: 112 us
  blocking collectives  87.3 us (77%)
  Pallas kernels  22.4 us (20%)
  starting transfers between devices  1.22 us (1%)
    all_to_all x5, blocking collectives, exchange(): return lax.all_to_all(x, axes, split_axis=0, concat_axis=0, tiled=True)  87.3 us
    pallas_call x12, Pallas kernels, call(): pl.pallas_call(body, out_shape=outs, in_specs=[VM] * len(args), out_specs...  20.2 us
  transfers between devices with their start and end apart: 4, of which 2 were waited for; matrix products, arithmetic and copies ran while one was open for 0% of the time, Pallas kernels for 6%

profile of v9, /device:TPU:0, one launch (start us, length us, event | category | flops | bytes accessed | tf_op | source)
XLA Modules:
  0.0 112.2 jit_solution(3094770279344692582)
XLA Ops:
  0.6 0.0 copy-start
  0.6 2.1 %shard_map.103 = (bf16[64,72,128]{2,1,0:T(8,128)(2,1)S(1)}, bf16[64,2048]{1,0:T(8,128)(2,1)S(1)}, bf16[512,2048]{1,0:T(8,128)(2,1)S(1)}) custom-call(bf16[2048,128]{1,0:T(8,128)(2,1)} %feat_hbm.1, s32[1,64]{1,0:T(1,128)} %bitcast.25, s32[1,512]{1,0:T(1,128)} %bitcast.24), custom_call_target="tpu_custom_call" | custom-call | flops 4831838208 | tf_op jit(solution)/shard_map/pallas_call | solution.py:90
  2.8 0.0 copy-start.1
  2.8 31.6 %all_to_all.25.got_ref = bf16[64,72,128]{2,1,0:T(8,128)(2,1)S(1)} all-to-all(bf16[64,72,128]{2,1,0:T(8,128)(2,1)S(1)} %get-tuple-element.18), channel_id=1, replica_groups=mesh['z'=4,'x'=4,'y'=4,'rep'=2] {'z','x','y'}, dimensions={0} | all-to-all | bytes 2359296 | tf_op jit(solution)/shard_map/all_to_all | solution.py:239
  34.4 0.0 copy-done
  34.4 3.8 %shard_map.105.part_ref = f32[1536,128]{1,0:T(8,128)S(1)} custom-call(bf16[64,72,128]{2,1,0:T(8,128)(2,1)S(1)} %all_to_all.25.got_ref, bf16[2048,4096]{1,0:T(8,128)(2,1)S(1)} %bitcast.8, bf16[2048,512]{1,0:T(8,128)(2,1)S(1)} %bitcast.14), custom_call_target="tpu_custom_call" | custom-call | flops 3623878656 | tf_op jit(solution)/shard_map/pallas_call | solution.py:33
  38.3 0.1 collective-permute-start.1
  38.4 1.4 %shard_map.104.part_ref = f32[512,128]{1,0:T(8,128)S(1)} custom-call(bf16[64,72,128]{2,1,0:T(8,128)(2,1)S(1)} %all_to_all.25.got_ref, bf16[2048,4096]{1,0:T(8,128)(2,1)S(1)} %bitcast.9, bf16[2048,512]{1,0:T(8,128)(2,1)S(1)} %bitcast.15), custom_call_target="tpu_custom_call" | custom-call | flops 1207959552 | tf_op jit(solution)/shard_map/pallas_call | solution.py:33
  39.8 0.6 collective-permute-start
  40.3 0.3 collective-permute-done.1.away_ref
  40.7 0.7 shard_map.106
  41.3 0.2 collective-permute-done.away_ref
  41.5 0.3 shard_map.107
  41.9 0.0 copy-start.3
  41.9 25.6 %all_to_all.26.got_ref = bf16[64,72,128]{2,1,0:T(8,128)(2,1)S(1)} all-to-all(bf16[64,72,128]{2,1,0:T(8,128)(2,1)S(1)} %shard_map.107), channel_id=1, replica_groups=mesh['z'=4,'x'=4,'y'=4,'rep'=2] {'z','x','y'}, dimensions={0} | all-to-all | bytes 2359296 | tf_op jit(solution)/shard_map/all_to_all | solution.py:239
  67.5 3.3 %shard_map.108 = (f32[1024,256]{1,0:T(8,128)S(1)}, bf16[4096,256]{1,0:T(8,128)(2,1)S(1)}, bf16[512,256]{1,0:T(8,128)(2,1)S(1)}) custom-call(bf16[64,72,128]{2,1,0:T(8,128)(2,1)S(1)} %all_to_all.26.got_ref, bf16[128,256]{1,0:T(8,128)(2,1)S(1)} %copy-done.3, bf16[2048,4096]{1,0:T(8,128)(2,1)S(1)} %bitcast.10, bf16[2048,512]{1,0:T(8,128)(2,1)S(1)} %bitcast.16), custom_call_target="tpu_custom_call" | custom-call | flops 2415919104 | tf_op jit(solution)/shard_map/pallas_call | solution.py:33
  70.7 0.1 collective-permute-start.2
  70.8 0.0 copy-start.2
  70.8 0.0 copy-start.4
  70.8 2.6 %shard_map.109.part_ref = f32[1024,256]{1,0:T(8,128)S(1)} custom-call(bf16[4096,256]{1,0:T(8,128)(2,1)S(1)} %get-tuple-element.23.hid_hub, bf16[512,256]{1,0:T(8,128)(2,1)S(1)} %get-tuple-element.24.hid_slot, bf16[2048,4096]{1,0:T(8,128)(2,1)S(1)} %bitcast.11, bf16[2048,512]{1,0:T(8,128)(2,1)S(1)} %bitcast.17), custom_call_target="tpu_custom_call" | custom-call | flops 2415919104 | tf_op jit(solution)/shard_map/pallas_call | solution.py:33
  73.4 0.0 collective-permute-done.2.away_ref
  73.5 0.0 copy-done.2
  73.5 1.2 %shard_map.110 = (bf16[172,1024]{1,0:T(8,128)(2,1)}, bf16[256,1024]{1,0:T(8,128)(2,1)S(1)}, f32[172,256]{1,0:T(8,128)S(1)}) custom-call(f32[1024,256]{1,0:T(8,128)S(1)} %shard_map.109.part_ref, f32[1024,256]{1,0:T(8,128)S(1)} %collective-permute-done.2.away_ref, bf16[172,256]{1,0:T(8,128)(2,1)S(1)} %bitcast.20, s32[1,1024]{1,0:T(1,128)S(1)} %bitcast.21), custom_call_target="tpu_custom_call" | custom-call | tf_op jit(solution)/shard_map/pallas_call | solution.py:33
  74.6 0.5 collective-permute-start.3
  75.1 2.6 %shard_map.111 = (f32[256,4096]{1,0:T(8,128)S(1)}, f32[256,512]{1,0:T(8,128)S(1)}) custom-call(bf16[256,1024]{1,0:T(8,128)(2,1)S(1)} %get-tuple-element.27.dsec_ref, bf16[2048,4096]{1,0:T(8,128)(2,1)S(1)} %bitcast.12, bf16[2048,512]{1,0:T(8,128)(2,1)S(1)} %bitcast.18), custom_call_target="tpu_custom_call" | custom-call | flops 2415919104 | tf_op jit(solution)/shard_map/pallas_call | solution.py:33
  77.7 0.0 collective-permute-done.3.dsec_ref
  77.7 3.6 %shard_map.112 = bf16[8,40,256]{2,1,0:T(8,128)(2,1)S(1)} custom-call(f32[256,4096]{1,0:T(8,128)S(1)} %get-tuple-element.28.hub_own, f32[256,512]{1,0:T(8,128)S(1)} %get-tuple-element.29.slot_own, f32[172,256]{1,0:T(8,128)S(1)} %get-tuple-element.30.grad_ref, bf16[256,1024]{1,0:T(8,128)(2,1)S(1)} %collective-permute-done.3.dsec_ref, ...), custom_call_target="tpu_custom_call" | custom-call | flops 2415919104 | tf_op jit(solution)/shard_map/pallas_call | solution.py:33
  81.3 8.9 %all_to_all.27.got_ref = bf16[8,40,256]{2,1,0:T(8,128)(2,1)S(1)} all-to-all(bf16[8,40,256]{2,1,0:T(8,128)(2,1)S(1)} %shard_map.112), channel_id=1, replica_groups=mesh['z'=4,'x'=4,'y'=4,'rep'=2] {'y','rep'}, dimensions={0} | all-to-all | bytes 327680 | tf_op jit(solution)/shard_map/all_to_all | solution.py:239
  90.2 12.4 %all_to_all.28.got_ref = bf16[16,40,256]{2,1,0:T(8,128)(2,1)S(1)} all-to-all(bf16[16,40,256]{2,1,0:T(8,128)(2,1)S(1)} %shard_map.113), channel_id=1, replica_groups=mesh['z'=4,'x'=4,'y'=4,'rep'=2] {'z','x'}, dimensions={0} | all-to-all | bytes 655360 | tf_op jit(solution)/shard_map/all_to_all | solution.py:239
  102.6 0.1 shard_map.114
  102.6 8.9 %all_to_all.29.got_ref = bf16[8,40,256]{2,1,0:T(8,128)(2,1)S(1)} all-to-all(bf16[8,40,256]{2,1,0:T(8,128)(2,1)S(1)} %shard_map.114), channel_id=1, replica_groups=mesh['z'=4,'x'=4,'y'=4,'rep'=2] {'y','rep'}, dimensions={0} | all-to-all | bytes 327680 | tf_op jit(solution)/shard_map/all_to_all | solution.py:239
  111.5 0.7 shard_map.115
  (4 shorter events, 0.0 us)
Async XLA Ops:
  0.6 33.8 %copy-start = (bf16[2048,1,4096]{2,0,1:T(8,128)(2,1)S(1)}, bf16[2048,1,4096]{2,0,1:T(8,128)(2,1)}, u32[]{:S(2)}) copy-start(bf16[2048,1,4096]{2,0,1:T(8,128)(2,1)} %param.14) | copy-start | bytes 50331652
  2.8 31.7 %copy-start.1 = (bf16[2048,1,512]{2,0,1:T(8,128)(2,1)S(1)}, bf16[2048,1,512]{2,0,1:T(8,128)(2,1)}, u32[]{:S(2)}) copy-start(bf16[2048,1,512]{2,0,1:T(8,128)(2,1)} %param.15) | copy-start | bytes 6291460
  38.3 2.4 %collective-permute-start.1 = (f32[1536,128]{1,0:T(8,128)S(1)}, f32[1536,128]{1,0:T(8,128)S(1)}, u32[]{:S(2)}, u32[]{:S(2)}) collective-permute-start(f32[1536,128]{1,0:T(8,128)S(1)} %shard_map.105.part_ref), channel_id=1, source_target_pairs={{0,1},{1,0},{2,3},{3,2},{4,5},{5,4},{6,7},{7,6},{8,9},{9,8},{10,11... | collective-permute-start | bytes 2359304 | tf_op jit(solution)/shard_map/ppermute | solution.py:242
  39.8 1.7 %collective-permute-start = (f32[512,128]{1,0:T(8,128)S(1)}, f32[512,128]{1,0:T(8,128)S(1)}, u32[]{:S(2)}, u32[]{:S(2)}) collective-permute-start(f32[512,128]{1,0:T(8,128)S(1)} %shard_map.104.part_ref), channel_id=1, source_target_pairs={{0,1},{1,0},{2,3},{3,2},{4,5},{5,4},{6,7},{7,6},{8,9},{9,8},{10,11... | collective-permute-start | bytes 786440 | tf_op jit(solution)/shard_map/ppermute | solution.py:242
  41.9 25.6 %copy-start.3 = (bf16[128,256]{1,0:T(8,128)(2,1)S(1)}, bf16[128,256]{1,0:T(8,128)(2,1)}, u32[]{:S(2)}) copy-start(bf16[128,256]{1,0:T(8,128)(2,1)} %w_ref.1) | copy-start | bytes 196612
  70.7 2.7 %collective-permute-start.2 = (f32[1024,256]{1,0:T(8,128)S(1)}, f32[1024,256]{1,0:T(8,128)S(1)}, u32[]{:S(2)}, u32[]{:S(2)}) collective-permute-start(f32[1024,256]{1,0:T(8,128)S(1)} %get-tuple-element.25), channel_id=1, source_target_pairs={{0,1},{1,0},{2,3},{3,2},{4,5},{5,4},{6,7},{7,6},{8,9},{9,8},{10,11... | collective-permute-start | bytes 3145736 | tf_op jit(solution)/shard_map/ppermute | solution.py:242
  70.8 2.6 %copy-start.2 = (bf16[256,172]{0,1:T(8,128)(2,1)S(1)}, bf16[256,172]{0,1:T(8,128)(2,1)}, u32[]{:S(2)}) copy-start(bf16[256,172]{0,1:T(8,128)(2,1)} %param.10) | copy-start | bytes 264196
  70.8 2.6 %copy-start.4 = (s32[1024]{0:T(1024)S(1)}, s32[1024]{0:T(1024)}, u32[]{:S(2)}) copy-start(s32[1024]{0:T(1024)} %param.11) | copy-start | bytes 12292
  74.6 3.1 %collective-permute-start.3 = (bf16[256,1024]{1,0:T(8,128)(2,1)S(1)}, bf16[256,1024]{1,0:T(8,128)(2,1)S(1)}, u32[]{:S(2)}, u32[]{:S(2)}) collective-permute-start(bf16[256,1024]{1,0:T(8,128)(2,1)S(1)} %get-tuple-element.27.dsec_ref), channel_id=1, source_target_pairs={{0,1},{1,0},{2,3},{3,2},{4,5},{5,4},{6,7},{7,6},{8,9},{9,8},{10,11... | collective-permute-start | bytes 1572872 | tf_op jit(solution)/shard_map/ppermute | solution.py:242
